TPU v7x, 32 devices: a whole 2x2x4 slice. The times are simulated.
32 devices in a mesh: expert: 8 (over z, x), shard: 4 (over y, core).
Axes of the slice: x: 2, y: 2, z: 4, core: 2. Of those that a mesh axis runs over, the one named last changes fastest.
Arguments:
- tokens: bfloat16 [4096, 2048], P(('expert', 'shard')), may hold values from -6 to 6
- first_gain: float32 [2048], replicated, may hold values from 0.25 to 1.75
- attention_in: bfloat16 [2048, 3, 2048], P('expert', None, 'shard'), may hold values from -0.125 to 0.125
- attention_bias: bfloat16 [3, 16, 128], P(None, 'shard', 'expert'), may hold values from -0.59765625 to 0.59765625
- attention_out: bfloat16 [2048, 2048], P('shard', 'expert'), may hold values from -0.5 to 0.5
- second_gain: float32 [2048], replicated, may hold values from 0.25 to 1.75
- router: bfloat16 [2048, 16], P('expert'), may hold values from -0.0625 to 0.0625
- shared_gate: bfloat16 [2048], P('expert'), may hold values from -0.125 to 0.125
- shared_in: bfloat16 [2048, 2, 5632], P('expert', None, 'shard'), may hold values from -0.125 to 0.125
- shared_out: bfloat16 [5632, 2048], P('shard', 'expert'), may hold values from -0.21875 to 0.21875
- expert_in: bfloat16 [16, 2048, 2, 1408], P('expert', None, None, 'shard'), may hold values from -0.125 to 0.125
- expert_out: bfloat16 [16, 1408, 2048], P('expert', 'shard'), may hold values from -4 to 4
- cotangent: bfloat16 [4096, 2048], P(('expert', 'shard')), may hold values from -6 to 6
- expert_picks: int32 [4096, 4], P(('expert', 'shard')), may hold values from 0 to 15, all different within a row; in each aligned block of 128 rows (0 to 127, 128 to 255, ...) at most 64 rows name the same one
Outputs:
- output: bfloat16 [4096, 2048], P(('expert', 'shard'))
- input_grad: float32 [4096, 2048], P(('expert', 'shard'))
- first_gain_grad: float32 [2048], replicated
- attention_in_grad: float32 [2048, 3, 2048], P('expert', None, 'shard')
- attention_bias_grad: float32 [3, 16, 128], P(None, 'shard', 'expert')
- attention_out_grad: float32 [2048, 2048], P('shard', 'expert')
- second_gain_grad: float32 [2048], replicated
- router_grad: float32 [2048, 16], P('expert')
- shared_gate_grad: float32 [2048], P('expert')
- shared_in_grad: float32 [2048, 2, 5632], P('expert', None, 'shard')
- shared_out_grad: float32 [5632, 2048], P('shard', 'expert')
- expert_in_grad: float32 [16, 2048, 2, 1408], P('expert', None, None, 'shard')
- expert_out_grad: float32 [16, 1408, 2048], P('expert', 'shard')
Inputs may be any that keep to these rules, and one draw needn't show every extreme that they name: `expert_picks`: each row names 4 different experts. Among the rows of one device no expert is named more than 64 times, and in every draw some device names some expert exactly 64 times.
All inputs are finite; a program needn't handle non-finite values.
Results may differ from a plain program's by a relative error of at most 0.03.
Values may be sent and summed in bfloat16 or wider, within the bound.
A program may use at most 320 MiB of HBM per device.

v0:
```python
import jax
import jax.numpy as jnp
from jax import lax
from jax.sharding import PartitionSpec as P

EPSILON = 1e-06
ROPE_BASE = 1000000.0
MASKED = -1e30


def normalize(activations):
    factor = lax.rsqrt(jnp.mean(activations * activations, axis=-1, keepdims=True) + EPSILON)
    return (activations * factor, factor)


def norm_back(incoming, normed, factor, gain_vec):
    scaled = incoming * gain_vec
    inner_mean = jnp.mean(scaled * normed, axis=-1, keepdims=True)
    return (factor * (scaled - normed * inner_mean), jnp.sum(incoming * normed, axis=0))


def rope_tables(length, head_dim):
    half_dim = head_dim // 2
    frequency = jnp.power(ROPE_BASE, -jnp.arange(half_dim, dtype=jnp.float32) * (2.0 / head_dim))
    angles = jnp.arange(length, dtype=jnp.float32)[:, None] * frequency[None, :]
    return (
        jnp.concatenate([jnp.cos(angles), jnp.cos(angles)], axis=-1),
        jnp.concatenate([jnp.sin(angles), jnp.sin(angles)], axis=-1),
    )


def rotate(values, cosine_table, sine_table):
    half_dim = values.shape[-1] // 2
    turned = jnp.concatenate([-values[..., half_dim:], values[..., :half_dim]], axis=-1)
    return values * cosine_table[:, None, :] + turned * sine_table[:, None, :]


def rotate_back(incoming, cosine_table, sine_table):
    half_dim = incoming.shape[-1] // 2
    scaled = incoming * sine_table[:, None, :]
    turned = jnp.concatenate([scaled[..., half_dim:], -scaled[..., :half_dim]], axis=-1)
    return incoming * cosine_table[:, None, :] + turned


def block_scores(query_block, keys_all, first_row, score_scale):
    scores = (
        jnp.einsum("qhd,khd->hqk", query_block, keys_all, preferred_element_type=jnp.float32)
        * score_scale
    )
    row_pos = first_row + jnp.arange(query_block.shape[0], dtype=jnp.int32)
    col_pos = jnp.arange(keys_all.shape[0], dtype=jnp.int32)
    return jnp.where(col_pos[None, None, :] <= row_pos[None, :, None], scores, MASKED)


def attend(queries, keys_all, values, block_rows, score_scale):
    blocks = queries.shape[0] // block_rows
    starts = jnp.arange(blocks, dtype=jnp.int32) * block_rows

    def one_block(block_item):
        query_block, first_row = block_item
        scores = block_scores(query_block, keys_all, first_row, score_scale)
        highest = jnp.max(scores, axis=-1, keepdims=True)
        raised = jnp.exp(scores - highest)
        row_total = jnp.sum(raised, axis=-1, keepdims=True)
        weights = (raised / row_total).astype(jnp.bfloat16)
        mixed_out = jnp.einsum("hqk,khd->qhd", weights, values, preferred_element_type=jnp.float32)
        return (mixed_out, (highest + jnp.log(row_total))[..., 0])

    shape_blocks = (blocks, block_rows) + queries.shape[1:]
    mixed_out, logsum = lax.map(one_block, (queries.reshape(shape_blocks), starts))
    return (mixed_out.reshape(queries.shape), logsum)


def attend_back(queries, keys_all, values, logsum, grad_out, block_rows, score_scale):
    blocks = queries.shape[0] // block_rows
    starts = jnp.arange(blocks, dtype=jnp.int32) * block_rows
    shape_blocks = (blocks, block_rows) + queries.shape[1:]

    def one_block(running, block_item):
        key_grad, value_grad = running
        query_block, grad_block, logsum_block, first_row = block_item
        scores = block_scores(query_block, keys_all, first_row, score_scale)
        block_probs = jnp.exp(scores - logsum_block[..., None])
        value_grad = value_grad + jnp.einsum(
            "hqk,qhd->khd",
            block_probs.astype(jnp.bfloat16),
            grad_block,
            preferred_element_type=jnp.float32,
        )
        prob_grad = jnp.einsum(
            "qhd,khd->hqk", grad_block, values, preferred_element_type=jnp.float32
        )
        score_grad = (
            block_probs * (prob_grad - jnp.sum(prob_grad * block_probs, axis=-1, keepdims=True))
        ).astype(jnp.bfloat16)
        query_grad = (
            jnp.einsum("hqk,khd->qhd", score_grad, keys_all, preferred_element_type=jnp.float32)
            * score_scale
        )
        key_grad = (
            key_grad
            + jnp.einsum(
                "hqk,qhd->khd", score_grad, query_block, preferred_element_type=jnp.float32
            )
            * score_scale
        )
        return ((key_grad, value_grad), query_grad)

    zero_keys = jnp.zeros(keys_all.shape, jnp.float32)
    (key_grad, value_grad), query_grad = lax.scan(
        one_block,
        (zero_keys, zero_keys),
        (queries.reshape(shape_blocks), grad_out.reshape(shape_blocks), logsum, starts),
    )
    return (query_grad.reshape(queries.shape), key_grad, value_grad)


def gate_up_forward(activations, weight_in, weight_out):
    raised = jnp.einsum(
        "rekd,edcf->rekcf", activations, weight_in, preferred_element_type=jnp.float32
    )
    hidden = (jax.nn.silu(raised[..., 0, :]) * raised[..., 1, :]).astype(jnp.bfloat16)
    result = jnp.einsum("rekf,efd->rekd", hidden, weight_out, preferred_element_type=jnp.float32)
    return (raised, hidden, result)


def gate_up_back(activations, weight_in, weight_out, raised, hidden, incoming):
    out_grad = jnp.einsum("rekf,rekd->efd", hidden, incoming, preferred_element_type=jnp.float32)
    hidden_grad = jnp.einsum(
        "rekd,efd->rekf", incoming, weight_out, preferred_element_type=jnp.float32
    )
    gate_part = raised[..., 0, :]
    up_part = raised[..., 1, :]
    sigmoid_gate = jax.nn.sigmoid(gate_part)
    gate_grad = (
        hidden_grad * up_part * sigmoid_gate * (1.0 + gate_part * (1.0 - sigmoid_gate))
    ).astype(jnp.bfloat16)
    up_grad = (hidden_grad * gate_part * sigmoid_gate).astype(jnp.bfloat16)
    gate_wgrad = jnp.einsum(
        "rekd,rekf->edf", activations, gate_grad, preferred_element_type=jnp.float32
    )
    up_wgrad = jnp.einsum(
        "rekd,rekf->edf", activations, up_grad, preferred_element_type=jnp.float32
    )
    both_grad = jnp.stack([gate_grad, up_grad], axis=-2)
    row_grad = jnp.einsum(
        "rekcf,edcf->rekd", both_grad, weight_in, preferred_element_type=jnp.float32
    )
    return (gate_wgrad, up_wgrad, out_grad, row_grad)


def local(
    tokens,
    first_gain,
    attention_in,
    attention_bias,
    attention_out,
    second_gain,
    router,
    shared_gate,
    shared_in,
    shared_out,
    expert_in,
    expert_out,
    cotangent,
    expert_picks,
):
    local_rows, model_width = tokens.shape
    shard_count = lax.axis_size("shard")
    owner_count = lax.axis_size("expert")
    seq_length = local_rows * shard_count
    expert_count = router.shape[1]
    pick_count = expert_picks.shape[1]
    owned_count = expert_in.shape[0]
    capacity = max(2, 2 * local_rows * pick_count // expert_count)
    heads_here = attention_bias.shape[1]
    head_dim = attention_bias.shape[2] * owner_count
    score_scale = head_dim ** (-0.5)
    block_rows = min(seq_length, 512)
    cosine_table, sine_table = rope_tables(seq_length, head_dim)

    def fetch_dense():
        return (
            lax.all_gather(attention_in, "expert", axis=0, tiled=True),
            lax.all_gather(attention_bias, "expert", axis=2, tiled=True),
            lax.all_gather(attention_out, "expert", axis=1, tiled=True),
            lax.all_gather(router, "expert", axis=0, tiled=True),
            lax.all_gather(shared_gate, "expert", axis=0, tiled=True),
            lax.all_gather(shared_in, "expert", axis=0, tiled=True),
            lax.all_gather(shared_out, "expert", axis=1, tiled=True),
        )

    def fetch_rows(normed_low):
        return (
            lax.all_gather(normed_low, "shard", axis=0, tiled=True),
            lax.all_gather(expert_in, "shard", axis=3, tiled=True),
            lax.all_gather(expert_out, "shard", axis=1, tiled=True),
        )

    inputs = tokens.astype(jnp.float32)
    first_norm, first_factor = normalize(inputs)
    first_low = (first_norm * first_gain).astype(jnp.bfloat16)
    att_in, att_bias, att_out, router_full, gate_full, shared_inw, shared_outw = fetch_dense()
    normed_all, expert_inw, expert_outw = fetch_rows(first_low)
    projected = jnp.einsum("sd,dcf->scf", normed_all, att_in, preferred_element_type=jnp.float32)
    projected = projected + att_bias.reshape(3, -1).astype(jnp.float32)[None]
    projected = projected.reshape(seq_length, 3, heads_here, head_dim)
    queries = rotate(projected[:, 0], cosine_table, sine_table).astype(jnp.bfloat16)
    keys_all = rotate(projected[:, 1], cosine_table, sine_table).astype(jnp.bfloat16)
    values = projected[:, 2].astype(jnp.bfloat16)
    attended, logsum = attend(queries, keys_all, values, block_rows, score_scale)
    attended_low = attended.astype(jnp.bfloat16).reshape(seq_length, -1)
    attn_part = jnp.dot(attended_low, att_out, preferred_element_type=jnp.float32)
    attn_local = lax.psum_scatter(
        attn_part.astype(jnp.bfloat16), "shard", scatter_dimension=0, tiled=True
    ).astype(jnp.float32)
    residual = inputs + attn_local
    second_norm, second_factor = normalize(residual)
    second_low = (second_norm * second_gain).astype(jnp.bfloat16)
    logits = jnp.dot(second_low, router_full, preferred_element_type=jnp.float32)
    route_probs = jax.nn.softmax(logits, axis=-1)
    picked = (
        expert_picks[:, :, None] == jnp.arange(expert_count, dtype=jnp.int32)[None, None, :]
    ).astype(jnp.float32)
    gate_values = jnp.sum(picked * route_probs[:, None, :], axis=-1)
    flat_picks = expert_picks.reshape(-1)
    flat_hot = (flat_picks[:, None] == jnp.arange(expert_count, dtype=jnp.int32)[None, :]).astype(
        jnp.int32
    )
    slot_ranks = jnp.sum((jnp.cumsum(flat_hot, axis=0) - flat_hot) * flat_hot, axis=1)
    slot_rows = flat_picks * capacity + slot_ranks
    outgoing = jnp.zeros((expert_count * capacity, model_width), jnp.bfloat16)
    outgoing = outgoing.at[slot_rows].set(jnp.repeat(second_low, pick_count, axis=0))
    arrived = lax.all_to_all(
        outgoing.reshape(owner_count, owned_count, capacity, model_width),
        "expert",
        split_axis=0,
        concat_axis=0,
        tiled=True,
    )
    mixed_all = lax.all_gather(second_low, "shard", axis=0, tiled=True)
    shared_raised, shared_hidden, shared_part = gate_up_forward(
        mixed_all[:, None, None, :], shared_inw[None], shared_outw[None]
    )
    shared_rows = lax.psum_scatter(
        shared_part[:, 0, 0, :].astype(jnp.bfloat16), "shard", scatter_dimension=0, tiled=True
    ).astype(jnp.float32)
    expert_raised, expert_hidden, expert_part = gate_up_forward(arrived, expert_inw, expert_outw)
    expert_result = expert_part.astype(jnp.bfloat16)
    shared_scale = jax.nn.sigmoid(
        jnp.dot(second_low, gate_full, preferred_element_type=jnp.float32)
    )
    out_grad = cotangent.astype(jnp.float32)
    slot_values = (
        (gate_values[:, :, None] * out_grad[:, None, :])
        .reshape(-1, model_width)
        .astype(jnp.bfloat16)
    )
    grad_send = (
        jnp.zeros((expert_count * capacity, model_width), jnp.bfloat16)
        .at[slot_rows]
        .set(slot_values)
    )
    returned, owner_grads = (
        lax.all_to_all(expert_result, "expert", split_axis=0, concat_axis=0, tiled=True),
        lax.all_to_all(
            grad_send.reshape(owner_count, owned_count, capacity, model_width),
            "expert",
            split_axis=0,
            concat_axis=0,
            tiled=True,
        ),
    )
    gathered_out = returned.reshape(expert_count * capacity, model_width)[slot_rows]
    gathered_out = gathered_out.reshape(local_rows, pick_count, model_width).astype(jnp.float32)
    routed = jnp.sum(gate_values[:, :, None] * gathered_out, axis=1)
    output = (residual + shared_scale[:, None] * shared_rows + routed).astype(jnp.bfloat16)
    pick_grad = jnp.sum(out_grad[:, None, :] * gathered_out, axis=-1)
    route_grad = jnp.sum(picked * pick_grad[:, :, None], axis=1)
    logit_grad = (
        route_probs * (route_grad - jnp.sum(route_grad * route_probs, axis=-1, keepdims=True))
    ).astype(jnp.bfloat16)
    scale_grad = jnp.sum(out_grad * shared_rows, axis=-1)
    gate_logit_grad = (scale_grad * shared_scale * (1.0 - shared_scale)).astype(jnp.bfloat16)
    shared_grad = (shared_scale[:, None] * out_grad).astype(jnp.bfloat16)
    shared_grad_all, logit_grad_all, gate_grad_all = (
        lax.all_gather(shared_grad, "shard", axis=0, tiled=True),
        lax.all_gather(logit_grad, "shard", axis=0, tiled=True),
        lax.all_gather(gate_logit_grad, "shard", axis=0, tiled=True),
    )
    att_in, att_bias, att_out, router_full, gate_full, shared_inw, shared_outw = fetch_dense()
    normed_all, expert_inw, expert_outw = fetch_rows(first_low)
    expert_gate_w, expert_up_w, expert_down_w, owner_row_grad = gate_up_back(
        arrived, expert_inw, expert_outw, expert_raised, expert_hidden, owner_grads
    )
    shared_gate_w, shared_up_w, shared_down_w, shared_row_grad = gate_up_back(
        mixed_all[:, None, None, :],
        shared_inw[None],
        shared_outw[None],
        shared_raised,
        shared_hidden,
        shared_grad_all[:, None, None, :],
    )
    owner_low = owner_row_grad.astype(jnp.bfloat16)
    shared_back = lax.psum_scatter(
        shared_row_grad[:, 0, 0, :].astype(jnp.bfloat16), "shard", scatter_dimension=0, tiled=True
    ).astype(jnp.float32)
    returned_grad = lax.all_to_all(owner_low, "expert", split_axis=0, concat_axis=0, tiled=True)
    routed_back = returned_grad.reshape(expert_count * capacity, model_width)[slot_rows]
    routed_back = jnp.sum(
        routed_back.reshape(local_rows, pick_count, model_width).astype(jnp.float32), axis=1
    )
    local_back = jnp.einsum(
        "te,de->td", logit_grad, router_full, preferred_element_type=jnp.float32
    )
    local_back = (
        local_back
        + gate_logit_grad.astype(jnp.float32)[:, None] * gate_full.astype(jnp.float32)[None, :]
    )
    second_grad = local_back + shared_back + routed_back
    residual_back, second_gain_grad = norm_back(
        second_grad, second_norm, second_factor, second_gain
    )
    residual_grad = out_grad + residual_back
    residual_all = lax.all_gather(residual_grad.astype(jnp.bfloat16), "shard", axis=0, tiled=True)
    att_out_grad = jnp.einsum(
        "sf,sd->fd", attended_low, residual_all, preferred_element_type=jnp.float32
    )
    attended_grad = jnp.einsum(
        "sd,fd->sf", residual_all, att_out, preferred_element_type=jnp.float32
    )
    attended_grad = attended_grad.astype(jnp.bfloat16).reshape(seq_length, heads_here, head_dim)
    query_grad, key_grad, value_grad = attend_back(
        queries, keys_all, values, logsum, attended_grad, block_rows, score_scale
    )
    projected_grad = jnp.stack(
        [
            rotate_back(query_grad, cosine_table, sine_table),
            rotate_back(key_grad, cosine_table, sine_table),
            value_grad,
        ],
        axis=1,
    )
    projected_grad = projected_grad.astype(jnp.bfloat16).reshape(
        seq_length, 3, heads_here * head_dim
    )
    att_in_grad = jnp.einsum(
        "sd,scf->dcf", normed_all, projected_grad, preferred_element_type=jnp.float32
    )
    att_bias_grad = jnp.sum(projected_grad.astype(jnp.float32), axis=0).reshape(
        3, heads_here, head_dim
    )
    first_part = jnp.einsum(
        "scf,dcf->sd", projected_grad, att_in, preferred_element_type=jnp.float32
    )
    first_grad, expert_gate_l, expert_up_l, expert_down_l = (
        lax.psum_scatter(
            first_part.astype(jnp.bfloat16), "shard", scatter_dimension=0, tiled=True
        ).astype(jnp.float32),
        lax.psum_scatter(
            expert_gate_w.astype(jnp.bfloat16), "shard", scatter_dimension=2, tiled=True
        ).astype(jnp.float32),
        lax.psum_scatter(
            expert_up_w.astype(jnp.bfloat16), "shard", scatter_dimension=2, tiled=True
        ).astype(jnp.float32),
        lax.psum_scatter(
            expert_down_w.astype(jnp.bfloat16), "shard", scatter_dimension=1, tiled=True
        ).astype(jnp.float32),
    )
    input_back, first_gain_grad = norm_back(first_grad, first_norm, first_factor, first_gain)
    input_grad = residual_grad + input_back
    router_grad = jnp.einsum(
        "sd,se->de", mixed_all, logit_grad_all, preferred_element_type=jnp.float32
    )
    gate_vec_grad = jnp.einsum(
        "sd,s->d", mixed_all, gate_grad_all, preferred_element_type=jnp.float32
    )
    shared_in_grad = jnp.stack([shared_gate_w[0], shared_up_w[0]], axis=1)
    (
        att_in_local,
        att_bias_local,
        att_out_local,
        router_local,
        gate_vec_local,
        shared_in_local,
        shared_out_local,
    ) = (
        lax.psum_scatter(
            att_in_grad.astype(jnp.bfloat16), "expert", scatter_dimension=0, tiled=True
        ).astype(jnp.float32),
        lax.psum_scatter(
            att_bias_grad.astype(jnp.bfloat16), "expert", scatter_dimension=2, tiled=True
        ).astype(jnp.float32),
        lax.psum_scatter(
            att_out_grad.astype(jnp.bfloat16), "expert", scatter_dimension=1, tiled=True
        ).astype(jnp.float32),
        lax.psum_scatter(
            router_grad.astype(jnp.bfloat16), "expert", scatter_dimension=0, tiled=True
        ).astype(jnp.float32),
        lax.psum_scatter(
            gate_vec_grad.astype(jnp.bfloat16), "expert", scatter_dimension=0, tiled=True
        ).astype(jnp.float32),
        lax.psum_scatter(
            shared_in_grad.astype(jnp.bfloat16), "expert", scatter_dimension=0, tiled=True
        ).astype(jnp.float32),
        lax.psum_scatter(
            shared_down_w[0].astype(jnp.bfloat16), "expert", scatter_dimension=1, tiled=True
        ).astype(jnp.float32),
    )
    first_gain_all, second_gain_all = lax.psum(
        (first_gain_grad, second_gain_grad), ("expert", "shard")
    )
    expert_in_grad = jnp.stack([expert_gate_l, expert_up_l], axis=2)
    return (
        output,
        input_grad,
        first_gain_all,
        att_in_local,
        att_bias_local,
        att_out_local,
        second_gain_all,
        router_local,
        gate_vec_local,
        shared_in_local,
        shared_out_local,
        expert_in_grad,
        expert_down_l,
    )


def solution(mesh):
    in_specs = (
        P(("expert", "shard"), None),
        P(),
        P("expert", None, "shard"),
        P(None, "shard", "expert"),
        P("shard", "expert"),
        P(),
        P("expert", None),
        P("expert"),
        P("expert", None, "shard"),
        P("shard", "expert"),
        P("expert", None, None, "shard"),
        P("expert", "shard", None),
        P(("expert", "shard"), None),
        P(("expert", "shard"), None),
    )
    out_specs = (
        P(("expert", "shard"), None),
        P(("expert", "shard"), None),
        P(),
        P("expert", None, "shard"),
        P(None, "shard", "expert"),
        P("shard", "expert"),
        P(),
        P("expert", None),
        P("expert"),
        P("expert", None, "shard"),
        P("shard", "expert"),
        P("expert", None, None, "shard"),
        P("expert", "shard", None),
    )
    return jax.shard_map(local, mesh=mesh, in_specs=in_specs, out_specs=out_specs, check_vma=False)
```

profile of v0, /device:TPU:0, one launch (start us, length us, event | category | flops | bytes accessed | tf_op | source)
XLA Modules:
  0.0 2087.5 jit_solution(17583457900610104787)
XLA Ops:
  14.4 32.3 %all_gather.56 = bf16[3,4,128]{1,0,2:T(4,128)(2,1)S(1)} all-gather(bf16[3,4,16]{1,0,2:T(4,128)(2,1)S(1)} %copy.214), channel_id=1, replica_groups=mesh['expert'=8,'shard'=4] {'expert'}, dimensions={2}, use_global_device_ids=true | all-gather | bytes 3456 | tf_op jit(solution)/shard_map/all_gather | solution.py:185
  48.4 90.7 %all-gather.15.cloned.1.call-done = bf16[2048,3,512]{0,2,1:T(8,128)(2,1)} async-done(((bf16[256,3,512]{0,2,1:T(8,128)(2,1)}), bf16[2048,3,512]{0,2,1:T(8,128)(2,1)}) %all-gather.15.cloned.1.call-update) | async-done | bytes 6291472 | tf_op jit(solution)/shard_map/all_gather | solution.py:184
  139.1 6.2 fusion.57
  150.9 39.6 %all-gather.17.cloned.1.call-done = bf16[512,2048]{1,0:T(8,128)(2,1)} async-done(((bf16[512,256]{1,0:T(8,128)(2,1)}), bf16[512,2048]{1,0:T(8,128)(2,1)}) %all-gather.17.cloned.1.call-update) | async-done | bytes 2097168 | tf_op jit(solution)/shard_map/all_gather | solution.py:186
  194.8 29.7 %reduce-scatter.16.cloned.1.call-done = bf16[128,2048]{1,0:T(8,128)(2,1)} async-done(((bf16[512,2048]{1,0:T(8,128)(2,1)}), bf16[128,2048]{1,0:T(8,128)(2,1)}) %reduce-scatter.16.cloned.1.call-update) | async-done | bytes 524304 | tf_op jit(solution)/shard_map/reduce_scatter | solution.py:214
  236.5 7.3 scatter_custom_fusion
  243.7 5.7 all-to-all-start
  257.8 167.8 %all_gather.62 = bf16[2048,16]{0,1:T(8,128)(2,1)S(1)} all-gather(bf16[256,16]{0,1:T(8,128)(2,1)S(1)} %copy-done.35), channel_id=1, replica_groups=mesh['expert'=8,'shard'=4] {'expert'}, dimensions={0}, use_global_device_ids=true | all-gather | bytes 73728 | tf_op jit(solution)/shard_map/all_gather | solution.py:187
  426.7 8.3 scatter_custom_fusion.1
  435.1 8.1 all-to-all-start.2
  444.0 107.4 %all-gather.21.cloned.1.call-done = bf16[2048,2,1408]{2,0,1:T(8,128)(2,1)} async-done(((bf16[256,2,1408]{2,0,1:T(8,128)(2,1)}), bf16[2048,2,1408]{2,0,1:T(8,128)(2,1)}) %all-gather.21.cloned.1.call-update) | async-done | bytes 11534352 | tf_op jit(solution)/shard_map/all_gather | solution.py:189
  551.4 12.7 convolution_bitcast_fusion
  564.1 131.3 %all-gather.25.cloned.1.call-done = bf16[2,2048,2,1408]{1,3,2,0:T(8,128)(2,1)} async-done(((bf16[2,2048,2,352]{1,3,2,0:T(8,128)(2,1)}), bf16[2,2048,2,1408]{1,3,2,0:T(8,128)(2,1)}) %all-gather.25.cloned.1.call-update) | async-done | bytes 23068688 | tf_op jit(solution)/shard_map/all_gather | solution.py:196
  695.5 20.6 fusion.10
  716.1 57.2 %all-gather.27.cloned.1.call-done = bf16[2,1408,2048]{2,1,0:T(8,128)(2,1)} async-done(((bf16[2,352,2048]{2,1,0:T(8,128)(2,1)}), bf16[2,1408,2048]{2,1,0:T(8,128)(2,1)}) %all-gather.27.cloned.1.call-update) | async-done | bytes 11534352 | tf_op jit(solution)/shard_map/all_gather | solution.py:197
  773.3 15.8 fusion.18
  789.0 19.7 fusion.2
  822.8 117.6 %all-gather.23.cloned.1.call-done = bf16[1408,2048]{1,0:T(8,128)(2,1)} async-done(((bf16[1408,256]{1,0:T(8,128)(2,1)}), bf16[1408,2048]{1,0:T(8,128)(2,1)}) %all-gather.23.cloned.1.call-update) | async-done | bytes 5767184 | tf_op jit(solution)/shard_map/all_gather | solution.py:190
  940.4 7.2 convolution_convert_fusion.6
  947.7 16.3 all-gather
  964.2 13.8 reduce-scatter.18.cloned.1.call-done
  980.2 10.4 convert_bitcast_fusion
  1002.9 9.1 fusion.36
  1013.1 10.1 bitcast_convert_fusion.5
  1024.4 7.5 gather_fusion.1
  1034.9 56.8 %all-to-all-done.1 = bf16[8,2,64,2048]{3,2,1,0:T(8,128)(2,1)} async-done(((bf16[8,2,64,2048]{3,2,1,0:T(8,128)(2,1)}), bf16[8,2,64,2048]{3,2,1,0:T(8,128)(2,1)}, u32[]{:S(2)}, u32[]{:S(2)}) %all-to-all-start.1) | async-done | bytes 4194336 | tf_op jit(solution)/shard_map/all_to_all | solution.py:265
  1091.7 7.1 gather_fusion
  1101.8 6.8 multiply_reduce_fusion.1
  1108.7 6.0 reduce_sum.181
  1118.5 7.8 convolution_convert_fusion
  1164.7 7.9 bitcast_convert_fusion.4
  1187.3 11.4 bitcast_convert_fusion.1
  1199.2 11.5 bitcast_convert_fusion.2
  1210.8 7.9 convolution_convert_fusion.3
  1218.8 11.4 bitcast_convert_fusion
  1239.2 21.8 %all-reduce = bf16[2048]{0:T(1024)(128)(2,1)S(1)} all-reduce(bf16[2048]{0:T(1024)(128)(2,1)S(1)} %convert_element_type.314), channel_id=10, replica_groups=mesh['expert'=8,'shard'=4] {'expert'}, use_global_device_ids=true, to_apply=%region_34.35.clone | all-reduce | flops 2048 | bytes 8192
  1263.9 47.3 %reduce-scatter.28.cloned.1.call-done = bf16[256,16]{0,1:T(8,128)(2,1)} async-done(((bf16[2048,16]{0,1:T(8,128)(2,1)}), bf16[256,16]{0,1:T(8,128)(2,1)}) %reduce-scatter.28.cloned.1.call-update) | async-done | bytes 8208 | tf_op jit(solution)/shard_map/reduce_scatter | solution.py:397
  1312.5 55.1 %reduce-scatter.40.cloned.1.call-done = bf16[16,12]{1,0:T(8,128)(2,1)} async-done(((bf16[128,12]{1,0:T(8,128)(2,1)}), bf16[16,12]{1,0:T(8,128)(2,1)}) %reduce-scatter.40.cloned.1.call-update) | async-done | bytes 400
  1369.1 69.8 %reduce-scatter.26.cloned.1.call-done = bf16[512,256]{1,0:T(8,128)(2,1)} async-done(((bf16[512,2048]{1,0:T(8,128)(2,1)}), bf16[512,256]{1,0:T(8,128)(2,1)}) %reduce-scatter.26.cloned.1.call-update) | async-done | bytes 262160 | tf_op jit(solution)/shard_map/reduce_scatter | solution.py:394
  1440.6 31.2 %reduce-scatter.22.cloned.1.call-done = bf16[128,2048]{1,0:T(8,128)(2,1)} async-done(((bf16[512,2048]{1,0:T(8,128)(2,1)}), bf16[128,2048]{1,0:T(8,128)(2,1)}) %reduce-scatter.22.cloned.1.call-update) | async-done | bytes 524304 | tf_op jit(solution)/shard_map/reduce_scatter | solution.py:357
  1473.3 43.7 %all-reduce.1 = (f32[2048]{0:T(1024)}, f32[2048]{0:T(1024)}) all-reduce(f32[2048]{0:T(1024)S(1)} %get-tuple-element.153, f32[2048]{0:T(1024)S(1)} %get-tuple-element.151), channel_id=1, replica_groups=mesh['expert'=8,'shard'=4] {'expert','shard'}, use_global_device_ids=true, to_apply=%region_26.27 | all-reduce | flops 4096 | bytes 32768 | tf_op jit(solution)/shard_map/psum | solution.py:410
  1520.3 150.8 %reduce-scatter.30.cloned.1.call-done = bf16[256,2,1408]{2,0,1:T(8,128)(2,1)} async-done(((bf16[2048,2,1408]{2,0,1:T(8,128)(2,1)}), bf16[256,2,1408]{2,0,1:T(8,128)(2,1)}) %reduce-scatter.30.cloned.1.call-update) | async-done | bytes 1441808 | tf_op jit(solution)/shard_map/reduce_scatter | solution.py:403
  1675.5 89.4 %reduce-scatter.36.cloned.1.call-done = bf16[2,2048,352]{1,2,0:T(8,128)(2,1)} async-done(((bf16[2,2048,1408]{1,2,0:T(8,128)(2,1)}), bf16[2,2048,352]{1,2,0:T(8,128)(2,1)}) %reduce-scatter.36.cloned.1.call-update) | async-done | bytes 2883600 | tf_op jit(solution)/shard_map/reduce_scatter | solution.py:363
  1764.9 94.8 %reduce-scatter.34.cloned.1.call-done = bf16[2,2048,352]{1,2,0:T(8,128)(2,1)} async-done(((bf16[2,2048,1408]{1,2,0:T(8,128)(2,1)}), bf16[2,2048,352]{1,2,0:T(8,128)(2,1)}) %reduce-scatter.34.cloned.1.call-update) | async-done | bytes 2883600 | tf_op jit(solution)/shard_map/reduce_scatter | solution.py:360
  1859.7 7.7 maximum_convert_fusion
  1867.5 11.2 copy.247
  1878.7 103.1 %reduce-scatter.24.cloned.1.call-done = bf16[256,3,512]{2,0,1:T(8,128)(2,1)} async-done(((bf16[2048,3,512]{2,0,1:T(8,128)(2,1)}), bf16[256,3,512]{2,0,1:T(8,128)(2,1)}) %reduce-scatter.24.cloned.1.call-update) | async-done | bytes 786448 | tf_op jit(solution)/shard_map/reduce_scatter | solution.py:388
  1984.2 91.5 %reduce-scatter.38.cloned.1.call-done = bf16[2,352,2048]{2,1,0:T(8,128)(2,1)} async-done(((bf16[2,1408,2048]{2,1,0:T(8,128)(2,1)}), bf16[2,352,2048]{2,1,0:T(8,128)(2,1)}) %reduce-scatter.38.cloned.1.call-update) | async-done | bytes 2883600 | tf_op jit(solution)/shard_map/reduce_scatter | solution.py:366
  (262 shorter events, 167.3 us)
Async XLA Ops:
  7.2 7.1 copy-start.42
  7.2 41.2 %all-gather.13.cloned.1.call-start = ((), (), s32[]{:S(2)}) async-start(), calls=%async_computation.17 | async-start | bytes 2621440 | tf_op jit(solution)/shard_map/all_gather | solution.py:195
  11.1 128.0 %all-gather.15.cloned.1.call-start = ((), (), s32[]{:S(2)}) async-start(), calls=%async_computation.18 | async-start | bytes 7077888 | tf_op jit(solution)/shard_map/all_gather | solution.py:184
  13.5 177.0 %all-gather.17.cloned.1.call-start = ((), (), s32[]{:S(2)}) async-start(), calls=%async_computation.19 | async-start | bytes 2359296 | tf_op jit(solution)/shard_map/all_gather | solution.py:186
  14.2 210.3 %reduce-scatter.16.cloned.1.call-start = ((), (), s32[]{:S(2)}) async-start(), calls=%async_computation.20 | async-start | bytes 2621440 | tf_op jit(solution)/shard_map/reduce_scatter | solution.py:214
  150.9 39.6 %copy-start.47 = (bf16[4,128,512]{2,1,0:T(8,128)(2,1)}, bf16[4,128,512]{2,1,0:T(8,128)(2,1)S(1)}, u32[]{:S(2)}) copy-start(bf16[4,128,512]{2,1,0:T(8,128)(2,1)S(1)} %fusion.71) | copy-start | bytes 1572868
  190.5 34.0 %copy-start.2 = (bf16[128,2048]{1,0:T(8,128)(2,1)S(1)}, bf16[128,2048]{1,0:T(8,128)(2,1)}, u32[]{:S(2)}) copy-start(bf16[128,2048]{1,0:T(8,128)(2,1)} %param.14) | copy-start | bytes 1572868
  190.5 35.9 %copy-start.24 = (f32[2048]{0:T(1024)S(1)}, f32[2048]{0:T(1024)}, u32[]{:S(2)}) copy-start(f32[2048]{0:T(1024)} %param.19) | copy-start | bytes 24580
  194.7 33.7 %copy-start.15 = (bf16[256,2,1408]{2,1,0:T(2,128)(2,1)S(1)}, bf16[256,2,1408]{2,1,0:T(2,128)(2,1)}, u32[]{:S(2)}) copy-start(bf16[256,2,1408]{2,1,0:T(2,128)(2,1)} %param.22) | copy-start | bytes 4325380
  194.8 249.2 %all-gather.19.cloned.1.call-start = ((), (), s32[]{:S(2)}) async-start(), calls=%async_computation.21 | async-start | bytes 2621440 | tf_op jit(solution)/shard_map/all_gather | solution.py:241
  228.4 323.0 %all-gather.21.cloned.1.call-start = ((), (), s32[]{:S(2)}) async-start(), calls=%async_computation.22 | async-start | bytes 12976128 | tf_op jit(solution)/shard_map/all_gather | solution.py:189
  229.7 465.7 %all-gather.25.cloned.1.call-start = ((), (), s32[]{:S(2)}) async-start(), calls=%async_computation.25 | async-start | bytes 28835840 | tf_op jit(solution)/shard_map/all_gather | solution.py:196
  230.5 542.8 %all-gather.27.cloned.1.call-start = ((), (), s32[]{:S(2)}) async-start(), calls=%async_computation.26 | async-start | bytes 14417920 | tf_op jit(solution)/shard_map/all_gather | solution.py:197
  243.7 191.3 %all-to-all-start = ((bf16[8,2,64,2048]{3,2,1,0:T(8,128)(2,1)}), bf16[8,2,64,2048]{3,2,1,0:T(8,128)(2,1)}, u32[]{:S(2)}, u32[]{:S(2)}) async-start(bf16[8,2,64,2048]{3,2,1,0:T(8,128)(2,1)} %bitcast.288), calls=%async_computation.2 | async-start | bytes 8388608 | tf_op jit(solution)/shard_map/all_to_all | solution.py:234
  425.9 9.1 copy-start.36
  426.6 8.4 copy-start.18
  435.1 338.2 %all-to-all-start.2 = ((bf16[8,2,64,2048]{3,2,1,0:T(8,128)(2,1)}), bf16[8,2,64,2048]{3,2,1,0:T(8,128)(2,1)}, u32[]{:S(2)}, u32[]{:S(2)}) async-start(bf16[8,2,64,2048]{3,2,1,0:T(8,128)(2,1)} %bitcast.286), calls=%async_computation.5 | async-start | bytes 8388608 | tf_op jit(solution)/shard_map/all_to_all | solution.py:266
  443.2 497.2 %all-gather.23.cloned.1.call-start = ((), (), s32[]{:S(2)}) async-start(), calls=%async_computation.23 | async-start | bytes 6488064 | tf_op jit(solution)/shard_map/all_gather | solution.py:190
  813.6 179.3 %all-to-all-start.3 = ((bf16[8,2,64,2048]{3,2,1,0:T(8,128)(2,1)}), bf16[8,2,64,2048]{3,2,1,0:T(8,128)(2,1)}, u32[]{:S(2)}, u32[]{:S(2)}) async-start(bf16[8,2,64,2048]{3,2,1,0:T(8,128)(2,1)} %bitcast.287), calls=%async_computation.6 | async-start | bytes 8388608 | tf_op jit(solution)/shard_map/all_to_all | solution.py:308
  819.1 158.9 %reduce-scatter.18.cloned.1.call-start = ((), (), s32[]{:S(2)}) async-start(), calls=%async_computation.24 | async-start | bytes 2621440 | tf_op jit(solution)/shard_map/reduce_scatter | solution.py:245
  822.8 124.8 %copy-start.14 = (bf16[512,1,1,1,1408]{4,0,3,2,1:T(8,128)(2,1)}, bf16[512,1,1,1,1408]{4,0,3,2,1:T(8,128)(2,1)S(1)}, u32[]{:S(2)}) copy-start(bf16[512,1,1,1,1408]{4,0,3,2,1:T(8,128)(2,1)S(1)} %multiply_convert_fusion.3) | copy-start | bytes 4325380
  822.8 124.9 %copy-start.43 = (bf16[256]{0:T(256)(128)(2,1)S(1)}, bf16[256]{0:T(256)(128)(2,1)}, u32[]{:S(2)}) copy-start(bf16[256]{0:T(256)(128)(2,1)} %param.21) | copy-start | bytes 1540
  947.6 55.3 %all-gather.29.cloned.1.call-start = ((), (), s32[]{:S(2)}) async-start(), calls=%async_computation.27 | async-start | bytes 2621440 | tf_op jit(solution)/shard_map/all_gather | solution.py:287
  992.9 98.8 %all-to-all-start.1 = ((bf16[8,2,64,2048]{3,2,1,0:T(8,128)(2,1)}), bf16[8,2,64,2048]{3,2,1,0:T(8,128)(2,1)}, u32[]{:S(2)}, u32[]{:S(2)}) async-start(bf16[8,2,64,2048]{3,2,1,0:T(8,128)(2,1)} %copy.227), calls=%async_computation.3 | async-start | bytes 8388608 | tf_op jit(solution)/shard_map/all_to_all | solution.py:265
  998.4 116.4 %reduce-scatter.20.cloned.1.call-start = ((), (), s32[]{:S(2)}) async-start(), calls=%async_computation.28 | async-start | bytes 2621440 | tf_op jit(solution)/shard_map/reduce_scatter | solution.py:305
  1012.0 11.2 copy-start.44
  1023.2 116.0 %all-gather.31.cloned.1.call-start = ((), (), s32[]{:S(2)}) async-start(), calls=%async_computation.29 | async-start | bytes 2621440 | tf_op jit(solution)/shard_map/all_gather | solution.py:325
  1108.6 6.1 copy-start.23
  1108.6 6.1 copy-start.34
  1108.6 6.1 copy-start.37
  1108.6 6.2 copy-start.3
  1108.6 6.2 copy-start.6
  1108.6 6.2 copy-start.21
  1108.6 6.2 copy-start.25
  1108.7 6.2 copy-start.39
  1118.2 143.4 %reduce-scatter.32.cloned.1.call-start = ((), (), s32[]{:S(2)}) async-start(), calls=%async_computation.35 | async-start | bytes 6488064 | tf_op jit(solution)/shard_map/reduce_scatter | solution.py:406
  1126.2 185.0 %reduce-scatter.28.cloned.1.call-start = ((), (), s32[]{:S(2)}) async-start(), calls=%async_computation.33 | async-start | bytes 73728 | tf_op jit(solution)/shard_map/reduce_scatter | solution.py:397
  1134.8 232.9 %reduce-scatter.40.cloned.1.call-start = ((), (), s32[]{:S(2)}) async-start(), calls=%async_computation.39 | async-start | bytes 36864
  1160.0 278.9 %reduce-scatter.26.cloned.1.call-start = ((), (), s32[]{:S(2)}) async-start(), calls=%async_computation.32 | async-start | bytes 2359296 | tf_op jit(solution)/shard_map/reduce_scatter | solution.py:394
  1164.5 307.4 %reduce-scatter.22.cloned.1.call-start = ((), (), s32[]{:S(2)}) async-start(), calls=%async_computation.30 | async-start | bytes 2621440 | tf_op jit(solution)/shard_map/reduce_scatter | solution.py:357
  1172.7 498.4 %reduce-scatter.30.cloned.1.call-start = ((), (), s32[]{:S(2)}) async-start(), calls=%async_computation.34 | async-start | bytes 12976128 | tf_op jit(solution)/shard_map/reduce_scatter | solution.py:403
  1187.2 577.7 %reduce-scatter.36.cloned.1.call-start = ((), (), s32[]{:S(2)}) async-start(), calls=%async_computation.37 | async-start | bytes 14417920 | tf_op jit(solution)/shard_map/reduce_scatter | solution.py:363
  1198.7 661.0 %reduce-scatter.34.cloned.1.call-start = ((), (), s32[]{:S(2)}) async-start(), calls=%async_computation.36 | async-start | bytes 14417920 | tf_op jit(solution)/shard_map/reduce_scatter | solution.py:360
  1210.7 771.0 %reduce-scatter.24.cloned.1.call-start = ((), (), s32[]{:S(2)}) async-start(), calls=%async_computation.31 | async-start | bytes 7077888 | tf_op jit(solution)/shard_map/reduce_scatter | solution.py:388
  1218.7 856.9 %reduce-scatter.38.cloned.1.call-start = ((), (), s32[]{:S(2)}) async-start(), calls=%async_computation.38 | async-start | bytes 14417920 | tf_op jit(solution)/shard_map/reduce_scatter | solution.py:366
  1230.3 241.6 %copy-start.26 = (f32[2048]{0:T(1024)S(1)}, f32[2048]{0:T(1024)}, u32[]{:S(2)}) copy-start(f32[2048]{0:T(1024)} %param.15) | copy-start | bytes 24580
  1230.3 241.6 %copy-start.41 = (f32[128]{0:T(128)S(1)}, f32[128]{0:T(128)}, u32[]{:S(2)}) copy-start(f32[128]{0:T(128)} %copy-done.40) | copy-start | bytes 1540
  1230.3 286.7 %copy-start.13 = (bf16[128,2048]{1,0:T(8,128)(2,1)S(1)}, bf16[128,2048]{1,0:T(8,128)(2,1)}, u32[]{:S(2)}) copy-start(bf16[128,2048]{1,0:T(8,128)(2,1)} %reduce-scatter.18.cloned.1.call-done) | copy-start | bytes 1572868
  (28 other events, 60.4 us)
Sparse Core Ops, SparseCore 0:
  11.2 25.2 all-gather.12
  39.2 99.9 all-gather.14
  141.2 49.2 all-gather.16
  194.9 29.5 reduce-scatter.15
  228.5 22.6 all-gather.18
  254.0 297.3 all-gather.20
  553.1 142.3 all-gather.24
  697.1 76.1 all-gather.26
  775.5 164.8 all-gather.22
  947.8 30.2 reduce-scatter.17
  980.3 22.5 all-gather.28
  1023.3 31.4 reduce-scatter.19
  1118.4 20.7 all-gather.30
  1143.7 110.6 reduce-scatter.31
  1257.7 53.4 reduce-scatter.27
  1315.1 52.5 reduce-scatter.39
  1371.4 67.3 reduce-scatter.25
  1441.4 30.4 reduce-scatter.21
  1476.0 195.0 reduce-scatter.29
  1673.5 91.3 reduce-scatter.35
  1767.5 92.1 reduce-scatter.33
  1863.3 118.3 reduce-scatter.23
  1984.3 91.3 reduce-scatter.37
where the time goes:
time: 2100 us; the launch traced here: 2090 us
  waiting for transfers between devices  1390 us (66%)
  blocking collectives  292 us (14%)
  matrix products  206 us (10%)
  local copies, waits for them, and re-layouts  81.9 us (4%)
  other arithmetic  76.5 us (4%)
  starting transfers between devices  26.7 us (1%)
    all_gather x1, blocking collectives, fetch_dense(): lax.all_gather(router, 'expert', axis=0, tiled=True)  168 us
    reduce_scatter x1, waiting for transfers between devices, local(): lax.psum_scatter(shared_in_grad.astype(jnp.bfloat16), 'expert', scatter_d...  151 us
    all_gather x1, waiting for transfers between devices, fetch_rows(): lax.all_gather(expert_in, 'shard', axis=3, tiled=True)  131 us
    all_gather x1, waiting for transfers between devices, fetch_dense(): lax.all_gather(shared_out, 'expert', axis=1, tiled=True)  118 us
    all_gather x1, waiting for transfers between devices, fetch_dense(): lax.all_gather(shared_in, 'expert', axis=0, tiled=True)  107 us
    reduce_scatter x1, waiting for transfers between devices, local(): lax.psum_scatter(att_in_grad.astype(jnp.bfloat16), 'expert', scatter_dime...  103 us
    reduce_scatter x1, waiting for transfers between devices, local(): lax.psum_scatter(expert_gate_w.astype(jnp.bfloat16), 'shard', scatter_dim...  94.8 us
    reduce_scatter x1, waiting for transfers between devices, local(): lax.psum_scatter(expert_down_w.astype(jnp.bfloat16), 'shard', scatter_dim...  91.5 us
  transfers between devices with their start and end apart: 27, of which 20 were waited for; matrix products, arithmetic and copies ran while one was open for 16% of the time, Pallas kernels for 0%

commit v1 on v0

--- a/solution.py
+++ b/solution.py
@@ -1,11 +1,18 @@
+import functools
+
 import jax
 import jax.numpy as jnp
 from jax import lax
+from jax.experimental import pallas as pl
+from jax.experimental.pallas import tpu as pltpu
 from jax.sharding import PartitionSpec as P
 
 EPSILON = 1e-06
 ROPE_BASE = 1000000.0
 MASKED = -1e30
+EXPERT, SHARD = "expert", "shard"
+CORE, ROW, COLUMN = "kc", "ky", "kx"
+SUM_CORES, SHARE, TOTAL = "sc", "share", "t"
 
 
 def normalize(activations):
@@ -149,7 +156,7 @@
     return (gate_wgrad, up_wgrad, out_grad, row_grad)
 
 
-def local(
+def local_exchange(
     tokens,
     first_gain,
     attention_in,
@@ -166,8 +173,8 @@
     expert_picks,
 ):
     local_rows, model_width = tokens.shape
-    shard_count = lax.axis_size("shard")
-    owner_count = lax.axis_size("expert")
+    shard_count = lax.axis_size(SHARD)
+    owner_count = lax.axis_size(EXPERT)
     seq_length = local_rows * shard_count
     expert_count = router.shape[1]
     pick_count = expert_picks.shape[1]
@@ -181,20 +188,20 @@
 
     def fetch_dense():
         return (
-            lax.all_gather(attention_in, "expert", axis=0, tiled=True),
-            lax.all_gather(attention_bias, "expert", axis=2, tiled=True),
-            lax.all_gather(attention_out, "expert", axis=1, tiled=True),
-            lax.all_gather(router, "expert", axis=0, tiled=True),
-            lax.all_gather(shared_gate, "expert", axis=0, tiled=True),
-            lax.all_gather(shared_in, "expert", axis=0, tiled=True),
-            lax.all_gather(shared_out, "expert", axis=1, tiled=True),
+            lax.all_gather(attention_in, EXPERT, axis=0, tiled=True),
+            lax.all_gather(attention_bias, EXPERT, axis=2, tiled=True),
+            lax.all_gather(attention_out, EXPERT, axis=1, tiled=True),
+            lax.all_gather(router, EXPERT, axis=0, tiled=True),
+            lax.all_gather(shared_gate, EXPERT, axis=0, tiled=True),
+            lax.all_gather(shared_in, EXPERT, axis=0, tiled=True),
+            lax.all_gather(shared_out, EXPERT, axis=1, tiled=True),
         )
 
     def fetch_rows(normed_low):
         return (
-            lax.all_gather(normed_low, "shard", axis=0, tiled=True),
-            lax.all_gather(expert_in, "shard", axis=3, tiled=True),
-            lax.all_gather(expert_out, "shard", axis=1, tiled=True),
+            lax.all_gather(normed_low, SHARD, axis=0, tiled=True),
+            lax.all_gather(expert_in, SHARD, axis=3, tiled=True),
+            lax.all_gather(expert_out, SHARD, axis=1, tiled=True),
         )
 
     inputs = tokens.astype(jnp.float32)
@@ -212,7 +219,7 @@
     attended_low = attended.astype(jnp.bfloat16).reshape(seq_length, -1)
     attn_part = jnp.dot(attended_low, att_out, preferred_element_type=jnp.float32)
     attn_local = lax.psum_scatter(
-        attn_part.astype(jnp.bfloat16), "shard", scatter_dimension=0, tiled=True
+        attn_part.astype(jnp.bfloat16), SHARD, scatter_dimension=0, tiled=True
     ).astype(jnp.float32)
     residual = inputs + attn_local
     second_norm, second_factor = normalize(residual)
@@ -233,17 +240,17 @@
     outgoing = outgoing.at[slot_rows].set(jnp.repeat(second_low, pick_count, axis=0))
     arrived = lax.all_to_all(
         outgoing.reshape(owner_count, owned_count, capacity, model_width),
-        "expert",
+        EXPERT,
         split_axis=0,
         concat_axis=0,
         tiled=True,
     )
-    mixed_all = lax.all_gather(second_low, "shard", axis=0, tiled=True)
+    mixed_all = lax.all_gather(second_low, SHARD, axis=0, tiled=True)
     shared_raised, shared_hidden, shared_part = gate_up_forward(
         mixed_all[:, None, None, :], shared_inw[None], shared_outw[None]
     )
     shared_rows = lax.psum_scatter(
-        shared_part[:, 0, 0, :].astype(jnp.bfloat16), "shard", scatter_dimension=0, tiled=True
+        shared_part[:, 0, 0, :].astype(jnp.bfloat16), SHARD, scatter_dimension=0, tiled=True
     ).astype(jnp.float32)
     expert_raised, expert_hidden, expert_part = gate_up_forward(arrived, expert_inw, expert_outw)
     expert_result = expert_part.astype(jnp.bfloat16)
@@ -262,10 +269,10 @@
         .set(slot_values)
     )
     returned, owner_grads = (
-        lax.all_to_all(expert_result, "expert", split_axis=0, concat_axis=0, tiled=True),
+        lax.all_to_all(expert_result, EXPERT, split_axis=0, concat_axis=0, tiled=True),
         lax.all_to_all(
             grad_send.reshape(owner_count, owned_count, capacity, model_width),
-            "expert",
+            EXPERT,
             split_axis=0,
             concat_axis=0,
             tiled=True,
@@ -284,9 +291,9 @@
     gate_logit_grad = (scale_grad * shared_scale * (1.0 - shared_scale)).astype(jnp.bfloat16)
     shared_grad = (shared_scale[:, None] * out_grad).astype(jnp.bfloat16)
     shared_grad_all, logit_grad_all, gate_grad_all = (
-        lax.all_gather(shared_grad, "shard", axis=0, tiled=True),
-        lax.all_gather(logit_grad, "shard", axis=0, tiled=True),
-        lax.all_gather(gate_logit_grad, "shard", axis=0, tiled=True),
+        lax.all_gather(shared_grad, SHARD, axis=0, tiled=True),
+        lax.all_gather(logit_grad, SHARD, axis=0, tiled=True),
+        lax.all_gather(gate_logit_grad, SHARD, axis=0, tiled=True),
     )
     att_in, att_bias, att_out, router_full, gate_full, shared_inw, shared_outw = fetch_dense()
     normed_all, expert_inw, expert_outw = fetch_rows(first_low)
@@ -303,9 +310,9 @@
     )
     owner_low = owner_row_grad.astype(jnp.bfloat16)
     shared_back = lax.psum_scatter(
-        shared_row_grad[:, 0, 0, :].astype(jnp.bfloat16), "shard", scatter_dimension=0, tiled=True
+        shared_row_grad[:, 0, 0, :].astype(jnp.bfloat16), SHARD, scatter_dimension=0, tiled=True
     ).astype(jnp.float32)
-    returned_grad = lax.all_to_all(owner_low, "expert", split_axis=0, concat_axis=0, tiled=True)
+    returned_grad = lax.all_to_all(owner_low, EXPERT, split_axis=0, concat_axis=0, tiled=True)
     routed_back = returned_grad.reshape(expert_count * capacity, model_width)[slot_rows]
     routed_back = jnp.sum(
         routed_back.reshape(local_rows, pick_count, model_width).astype(jnp.float32), axis=1
@@ -322,7 +329,7 @@
         second_grad, second_norm, second_factor, second_gain
     )
     residual_grad = out_grad + residual_back
-    residual_all = lax.all_gather(residual_grad.astype(jnp.bfloat16), "shard", axis=0, tiled=True)
+    residual_all = lax.all_gather(residual_grad.astype(jnp.bfloat16), SHARD, axis=0, tiled=True)
     att_out_grad = jnp.einsum(
         "sf,sd->fd", attended_low, residual_all, preferred_element_type=jnp.float32
     )
@@ -355,16 +362,16 @@
     )
     first_grad, expert_gate_l, expert_up_l, expert_down_l = (
         lax.psum_scatter(
-            first_part.astype(jnp.bfloat16), "shard", scatter_dimension=0, tiled=True
+            first_part.astype(jnp.bfloat16), SHARD, scatter_dimension=0, tiled=True
         ).astype(jnp.float32),
         lax.psum_scatter(
-            expert_gate_w.astype(jnp.bfloat16), "shard", scatter_dimension=2, tiled=True
+            expert_gate_w.astype(jnp.bfloat16), SHARD, scatter_dimension=2, tiled=True
         ).astype(jnp.float32),
         lax.psum_scatter(
-            expert_up_w.astype(jnp.bfloat16), "shard", scatter_dimension=2, tiled=True
+            expert_up_w.astype(jnp.bfloat16), SHARD, scatter_dimension=2, tiled=True
         ).astype(jnp.float32),
         lax.psum_scatter(
-            expert_down_w.astype(jnp.bfloat16), "shard", scatter_dimension=1, tiled=True
+            expert_down_w.astype(jnp.bfloat16), SHARD, scatter_dimension=1, tiled=True
         ).astype(jnp.float32),
     )
     input_back, first_gain_grad = norm_back(first_grad, first_norm, first_factor, first_gain)
@@ -386,29 +393,29 @@
         shared_out_local,
     ) = (
         lax.psum_scatter(
-            att_in_grad.astype(jnp.bfloat16), "expert", scatter_dimension=0, tiled=True
+            att_in_grad.astype(jnp.bfloat16), EXPERT, scatter_dimension=0, tiled=True
         ).astype(jnp.float32),
         lax.psum_scatter(
-            att_bias_grad.astype(jnp.bfloat16), "expert", scatter_dimension=2, tiled=True
+            att_bias_grad.astype(jnp.bfloat16), EXPERT, scatter_dimension=2, tiled=True
         ).astype(jnp.float32),
         lax.psum_scatter(
-            att_out_grad.astype(jnp.bfloat16), "expert", scatter_dimension=1, tiled=True
+            att_out_grad.astype(jnp.bfloat16), EXPERT, scatter_dimension=1, tiled=True
         ).astype(jnp.float32),
         lax.psum_scatter(
-            router_grad.astype(jnp.bfloat16), "expert", scatter_dimension=0, tiled=True
+            router_grad.astype(jnp.bfloat16), EXPERT, scatter_dimension=0, tiled=True
         ).astype(jnp.float32),
         lax.psum_scatter(
-            gate_vec_grad.astype(jnp.bfloat16), "expert", scatter_dimension=0, tiled=True
+            gate_vec_grad.astype(jnp.bfloat16), EXPERT, scatter_dimension=0, tiled=True
         ).astype(jnp.float32),
         lax.psum_scatter(
-            shared_in_grad.astype(jnp.bfloat16), "expert", scatter_dimension=0, tiled=True
+            shared_in_grad.astype(jnp.bfloat16), EXPERT, scatter_dimension=0, tiled=True
         ).astype(jnp.float32),
         lax.psum_scatter(
-            shared_down_w[0].astype(jnp.bfloat16), "expert", scatter_dimension=1, tiled=True
+            shared_down_w[0].astype(jnp.bfloat16), EXPERT, scatter_dimension=1, tiled=True
         ).astype(jnp.float32),
     )
     first_gain_all, second_gain_all = lax.psum(
-        (first_gain_grad, second_gain_grad), ("expert", "shard")
+        (first_gain_grad, second_gain_grad), (EXPERT, SHARD)
     )
     expert_in_grad = jnp.stack([expert_gate_l, expert_up_l], axis=2)
     return (
@@ -428,36 +435,1295 @@
     )
 
 
+MESH = pl.DeviceIdType.MESH
+EXTRA = 128
+NT_DIMS = (((1,), (1,)), ((), ()))
+
+
+class Place:
+    def __init__(self):
+        e, s = lax.axis_index(EXPERT), lax.axis_index(SHARD)
+        self.z, self.x, self.y, self.c = e // 2, e % 2, s // 2, s % 2
+
+    def z_of(self, kz):
+        z = self.z
+        return (z, z + 1 - 2 * (z % 2), (z + 2) % 4, 3 - z)[kz]
+
+    def x_of(self, kx):
+        return (self.x, 1 - self.x)[kx]
+
+    def y_of(self, ky):
+        return (self.y, 1 - self.y)[ky]
+
+    def c_of(self, kc):
+        return (self.c, 1 - self.c)[kc]
+
+    def device(self, kz=0, kx=0, ky=0, kc=0):
+        return (self.z_of(kz) * 2 + self.x_of(kx), self.y_of(ky) * 2 + self.c_of(kc))
+
+    def sequence(self, kz, kx):
+        return self.z_of(kz) * 2 + self.x_of(kx)
+
+    def block(self, kz, kx, ky, kc):
+        return self.sequence(kz, kx) * 4 + self.y_of(ky) * 2 + self.c_of(kc)
+
+
+PARTNERS = [dict(kz=1), dict(kz=2), dict(kz=3), dict(kx=1), dict(ky=1), dict(kc=1)]
+FARTHER = [dict(kz=1, kx=1), dict(kz=2, kx=1), dict(kz=3, kx=1)]
+
+
+def greet(place, partners):
+    barrier = pltpu.get_barrier_semaphore()
+    for partner in partners:
+        pl.semaphore_signal(
+            barrier, inc=1, device_id=place.device(**partner), device_id_type=MESH
+        )
+    pl.semaphore_wait(barrier, len(partners))
+
+
+class Copies:
+    def __init__(self, place, send_sems, recv_sems):
+        self.place, self.send_sems, self.recv_sems = place, send_sems, recv_sems
+        self.made = {}
+
+    def start(self, name, source, target, **partner):
+        at = len(self.made)
+        copy = pltpu.make_async_remote_copy(
+            src_ref=source,
+            dst_ref=target,
+            send_sem=self.send_sems.at[at],
+            recv_sem=self.recv_sems.at[at],
+            device_id=self.place.device(**partner),
+            device_id_type=MESH,
+        )
+        copy.start()
+        self.made[name] = copy
+
+    def arrived(self, name):
+        self.made[name].wait_recv()
+
+    def sent(self, name):
+        self.made[name].wait_send()
+
+
+GATHER_COPIES = 55
+SUM_COPIES = 43
+
+
+class Gather:
+    def __init__(self, place, copies, block_ref, all_ref, rows):
+        self.place, self.copies = place, copies
+        self.block_ref, self.all_ref, self.rows = block_ref, all_ref, rows
+
+    def view(self, kz, kx, ky, piece, own=False):
+        half = self.rows // 2
+        first = 0 if piece in (None, 0) else half
+        count = self.rows if piece is None else half
+        if own and (kz, kx, ky) == (0, 0, 0):
+            return self.block_ref.at[pl.ds(first, count)]
+        start = self.place.block(kz, kx, ky, 0) * self.rows + first
+        return self.all_ref.at[pl.ds(pl.multiple_of(start, half), count)]
+
+    def send(self, name, from_z, from_x, from_y, piece, **partner):
+        self.copies.start(
+            name,
+            self.view(from_z, from_x, from_y, piece, own=True),
+            self.view(from_z, from_x, from_y, piece),
+            **partner,
+        )
+
+    def begin(self, kz):
+        self.send(("z", kz), 0, 0, 0, None, kz=kz)
+
+    def first(self, kz):
+        if kz:
+            self.copies.arrived(("z", kz))
+        self.send(("y0", kz, 0), kz, 0, 0, 0, ky=1)
+        self.send(("y1", kz), kz, 0, 0, 1, ky=1)
+        self.send(("x0", kz), kz, 0, 0, 0, kx=1)
+        self.send(("x1", kz, 0), kz, 0, 0, 1, kx=1)
+        self.send(("c", kz), kz, 0, 0, None, kc=1)
+
+    def second_y(self, kz):
+        self.copies.arrived(("y1", kz))
+        self.send(("x1", kz, 1), kz, 0, 1, 1, kx=1)
+        self.send(("c01", kz), kz, 0, 1, 1, kc=1)
+        self.copies.arrived(("y0", kz, 0))
+        self.send(("c00", kz), kz, 0, 1, 0, kc=1)
+
+    def second_x(self, kz):
+        self.copies.arrived(("x0", kz))
+        self.send(("y0", kz, 1), kz, 1, 0, 0, ky=1)
+        self.send(("c10", kz), kz, 1, 0, 0, kc=1)
+        self.copies.arrived(("x1", kz, 0))
+        self.send(("c11", kz), kz, 1, 0, 1, kc=1)
+
+    def third(self, kz):
+        self.copies.arrived(("y0", kz, 1))
+        self.send(("c20", kz), kz, 1, 1, 0, kc=1)
+        self.copies.arrived(("x1", kz, 1))
+        self.send(("c21", kz), kz, 1, 1, 1, kc=1)
+
+    def have(self, kz, kx):
+        for name in ("c10", "c11", "c20", "c21") if kx else ("c", "c00", "c01"):
+            self.copies.arrived((name, kz))
+
+
+class Sums:
+    def __init__(self, place, copies, tag, held, from_y0, from_y1, from_x0, from_x1, from_z):
+        self.place, self.copies, self.tag, self.held = place, copies, tag, held
+        self.from_y0, self.from_y1 = from_y0, from_y1
+        self.from_x0, self.from_x1, self.from_z = from_x0, from_x1, from_z
+        self.rows = held.shape[1]
+        self.half = self.rows // 2
+
+    def slot(self, kz, kx, ky, piece=None):
+        at = kz * 4 + kx * 2 + ky
+        if piece is None:
+            return self.held.at[at]
+        return self.held.at[at, pl.ds(piece * self.half, self.half)]
+
+    def staged_part(self, staged):
+        def view(ky, kc):
+            start = (self.place.y_of(ky) * 2 + self.place.c_of(kc)) * self.rows
+            return staged.at[pl.ds(pl.multiple_of(start, self.rows), self.rows)]
+
+        return view
+
+    def add(self, into, other):
+        into[...] = into[...] + other[...]
+
+    def cores(self, kz, kx, part):
+        for ky in (1, 0):
+            self.copies.start((SUM_CORES, self.tag, kz, kx, ky), part(ky, 1), self.slot(kz, kx, ky), kc=1)
+
+    def first(self, kz, kx, part):
+        for ky in (1, 0):
+            self.copies.arrived((SUM_CORES, self.tag, kz, kx, ky))
+            self.add(self.slot(kz, kx, ky), part(ky, 0))
+            if ky:
+                self.copies.start(
+                    ("sy0", self.tag, kz, kx), self.slot(kz, kx, 1, 0), self.from_y0.at[kz * 2 + kx], ky=1
+                )
+            if kx:
+                self.copies.start(
+                    ("sx1", self.tag, kz, ky), self.slot(kz, 1, ky, 1), self.from_x1.at[kz * 2 + ky], kx=1
+                )
+        for ky in (1, 0):
+            self.copies.sent((SUM_CORES, self.tag, kz, kx, ky))
+
+    def second_away(self, kz):
+        self.copies.arrived(("sy0", self.tag, kz, 1))
+        self.add(self.slot(kz, 1, 0, 0), self.from_y0.at[kz * 2 + 1])
+        self.copies.start(("sx0", self.tag, kz), self.slot(kz, 1, 0, 0), self.from_x0.at[kz], kx=1)
+
+    def second_here(self, kz):
+        self.copies.arrived(("sx1", self.tag, kz, 1))
+        self.add(self.slot(kz, 0, 1, 1), self.from_x1.at[kz * 2 + 1])
+        self.copies.start(("sy1", self.tag, kz), self.slot(kz, 0, 1, 1), self.from_y1.at[kz], ky=1)
+        self.copies.arrived(("sx1", self.tag, kz, 0))
+        self.add(self.slot(kz, 0, 0, 1), self.from_x1.at[kz * 2])
+        self.copies.arrived(("sy0", self.tag, kz, 0))
+        self.add(self.slot(kz, 0, 0, 0), self.from_y0.at[kz * 2])
+        self.copies.arrived(("sx0", self.tag, kz))
+        self.add(self.slot(kz, 0, 0, 0), self.from_x0.at[kz])
+
+    def third(self, kz):
+        self.copies.arrived(("sy1", self.tag, kz))
+        self.add(self.slot(kz, 0, 0, 1), self.from_y1.at[kz])
+        if kz:
+            self.copies.start(("sz", self.tag, kz), self.slot(kz, 0, 0), self.from_z.at[kz - 1], kz=kz)
+
+    def total(self):
+        total = self.slot(0, 0, 0)[...].astype(jnp.float32)
+        for kz in (1, 2, 3):
+            self.copies.arrived(("sz", self.tag, kz))
+            total = total + self.from_z.at[kz - 1][...].astype(jnp.float32)
+        return total
+
+
+def mixture_kernel(
+    sizes,
+    block_ref,
+    cot_ref,
+    expert_in_ref,
+    shared_in_ref,
+    expert_out_ref,
+    shared_out_ref,
+    select_ref,
+    place_ref,
+    residual_ref,
+    output_ref,
+    sum_ref,
+    rows_ref,
+    units_ref,
+    weight_in,
+    weight_out,
+    rows_buf,
+    cot_buf,
+    units_buf,
+    dots,
+    staged_out,
+    staged_back,
+    *rest,
+):
+    rows, seq, width, owned, part, shared_part, padded = sizes
+    out_slots, back_slots = rest[:6], rest[6:12]
+    send_sems, recv_sems, load_sems, misc_sems = rest[12:]
+    bf16, f32 = jnp.bfloat16, jnp.float32
+    place = Place()
+    copies = Copies(place, send_sems, recv_sems)
+    gather = Gather(place, copies, block_ref, rows_ref, rows)
+    sums_out = Sums(place, copies, 0, *out_slots)
+    sums_back = Sums(place, copies, 1, *back_slots)
+    both = (sums_out, sums_back)
+
+    own = pltpu.make_async_copy(block_ref, gather.view(0, 0, 0, None), misc_sems.at[0])
+    own.start()
+    moves = []
+    for c in (0, 1):
+        for e in range(owned):
+            moves.append(
+                (
+                    expert_in_ref.at[pl.ds((2 * e + c) * part, part)],
+                    weight_in.at[pl.ds(c * padded + e * part, part)],
+                )
+            )
+        moves.append(
+            (
+                shared_in_ref.at[pl.ds(c * shared_part, shared_part)],
+                weight_in.at[pl.ds(c * padded + owned * part, shared_part)],
+            )
+        )
+    moves.append((expert_out_ref, weight_out.at[pl.ds(0, owned * part)]))
+    moves.append((shared_out_ref, weight_out.at[pl.ds(owned * part, shared_part)]))
+    loads = [
+        pltpu.make_async_copy(source, target, load_sems.at[i])
+        for i, (source, target) in enumerate(moves)
+    ]
+    for load in loads:
+        load.start()
+
+    order = [(0, 1), (1, 1), (1, 0), (2, 1), (2, 0), (3, 1), (3, 0), (0, 0)]
+
+    def span(step):
+        return pl.ds(pl.multiple_of(place.sequence(*order[step]) * seq, seq), seq)
+
+    def rows_load(step):
+        return pltpu.make_async_copy(rows_ref.at[span(step)], rows_buf, misc_sems.at[1])
+
+    def cot_load(step):
+        return pltpu.make_async_copy(cot_ref.at[span(step)], cot_buf, misc_sems.at[2])
+
+    def units_write(step):
+        return pltpu.make_async_copy(units_buf, units_ref.at[span(step)], misc_sems.at[3])
+
+    cot_load(0).start()
+    greet(place, PARTNERS)
+    gather.first(0)
+    gather.begin(1)
+    used = owned * part + shared_part
+    for at in (used, padded + used):
+        weight_in[pl.ds(at, padded - used), :] = jnp.zeros((padded - used, width), bf16)
+    weight_out[pl.ds(used, padded - used), :] = jnp.zeros((padded - used, width), bf16)
+    gather.second_x(0)
+    gather.second_y(0)
+    gather.begin(2)
+    gather.third(0)
+    gather.first(1)
+    own.wait()
+    gather.have(0, 1)
+    rows_load(0).start()
+    for load in loads:
+        load.wait()
+
+    def raise_tile(at, count):
+        here, above = pl.ds(at, count), pl.ds(at + padded, count)
+        pair = jnp.concatenate([weight_in[here, :], weight_in[above, :]], axis=0)
+        raised = lax.dot_general(
+            rows_buf[:, pl.ds(0, width)], pair, NT_DIMS, preferred_element_type=f32
+        )
+        back = lax.dot_general(
+            cot_buf[...], weight_out[here, :], NT_DIMS, preferred_element_type=f32
+        )
+        scale = jnp.dot(
+            rows_buf[:, pl.ds(width, EXTRA)], select_ref[:, here], preferred_element_type=f32
+        )
+        gate, up = raised[:, :count], raised[:, count:]
+        sigmoid_gate = jax.nn.sigmoid(gate)
+        active = gate * sigmoid_gate
+        hidden = active * up
+        dots[...] += jnp.dot(
+            (back * hidden).astype(bf16), place_ref[here, :], preferred_element_type=f32
+        )
+        scaled = back * scale
+        units_buf[:, pl.ds(at + 2 * padded, count)] = (hidden * scale).astype(bf16)
+        units_buf[:, here] = (
+            scaled * up * sigmoid_gate * (1.0 + gate * (1.0 - sigmoid_gate))
+        ).astype(bf16)
+        units_buf[:, above] = (scaled * active).astype(bf16)
+
+    tile, wide = 256, 512
+
+    def raise_and_back():
+        dots[...] = jnp.zeros_like(dots)
+
+        @pl.loop(0, padded // tile)
+        def _(j):
+            raise_tile(pl.multiple_of(j * tile, tile), tile)
+
+        if padded % tile:
+            raise_tile(padded // tile * tile, padded % tile)
+
+    def project_out():
+        @pl.loop(0, width // wide)
+        def _(n):
+            at = pl.ds(pl.multiple_of(n * wide, wide), wide)
+            staged_out[:, at] = jnp.dot(
+                units_buf[:, pl.ds(2 * padded, padded)],
+                weight_out[:, at],
+                preferred_element_type=f32,
+            ).astype(bf16)
+
+    def project_back():
+        @pl.loop(0, width // wide)
+        def _(n):
+            at = pl.ds(pl.multiple_of(n * wide, wide), wide)
+            staged_back[:, at] = jnp.dot(
+                units_buf[:, pl.ds(0, 2 * padded)], weight_in[:, at], preferred_element_type=f32
+            ).astype(bf16)
+
+        staged_back[:, pl.ds(width, EXTRA)] = dots[...].astype(bf16)
+
+    def sums_first(done):
+        sums_out.first(*order[done], sums_out.staged_part(staged_out))
+        sums_back.first(*order[done], sums_back.staged_part(staged_back))
+
+    def second_gather(kz):
+        gather.second_y(kz)
+        gather.second_x(kz)
+
+    def next_rows(step):
+        if step + 1 < len(order):
+            gather.have(*order[step + 1])
+            rows_load(step + 1).start()
+
+    def after_raise(step):
+        if step:
+            sums_first(step - 1)
+        if step == 0:
+            second_gather(1)
+            gather.begin(3)
+        elif step == 1:
+            gather.first(2)
+        elif step == 2:
+            gather.third(2)
+            gather.first(3)
+            for sums in both:
+                sums.second_away(0)
+        elif step == 3:
+            second_gather(3)
+            for sums in both:
+                sums.second_away(1)
+        elif step == 4:
+            gather.third(3)
+            for sums in both:
+                sums.second_here(1)
+        elif step == 5:
+            for sums in both:
+                sums.second_away(2)
+            for sums in both:
+                sums.third(1)
+        elif step == 6:
+            for sums in both:
+                sums.second_here(2)
+        elif step == 7:
+            for sums in both:
+                sums.second_away(3)
+            for sums in both:
+                sums.third(2)
+
+    def after_out(step):
+        if step == 0:
+            gather.third(1)
+        else:
+            next_rows(step)
+
+    def after_back(step):
+        if step == 0:
+            next_rows(step)
+        elif step == 1:
+            second_gather(2)
+        elif step == 7:
+            for sums in both:
+                sums.second_here(3)
+
+    for step in range(len(order)):
+        rows_load(step).wait()
+        cot_load(step).wait()
+        if step:
+            units_write(step - 1).wait()
+        raise_and_back()
+        units_write(step).start()
+        if step + 1 < len(order):
+            cot_load(step + 1).start()
+        after_raise(step)
+        project_out()
+        sums_out.cores(*order[step], sums_out.staged_part(staged_out))
+        after_out(step)
+        project_back()
+        sums_back.cores(*order[step], sums_back.staged_part(staged_back))
+        after_back(step)
+    last = len(order) - 1
+    sums_first(last)
+    for sums in both:
+        sums.third(3)
+    for sums in both:
+        sums.second_here(0)
+    for sums in both:
+        sums.third(0)
+    output_ref[...] = (residual_ref[...] + sums_out.total()).astype(bf16)
+    sum_ref[...] = sums_back.total()
+    units_write(last).wait()
+    for name in copies.made:
+        if name[0] != SUM_CORES:
+            copies.sent(name)
+
+
+def sum_slots(rows, packed):
+    half = rows // 2
+    bf16 = jnp.bfloat16
+    return [
+        pltpu.VMEM((16, rows, packed), bf16),
+        pltpu.VMEM((8, half, packed), bf16),
+        pltpu.VMEM((4, half, packed), bf16),
+        pltpu.VMEM((4, half, packed), bf16),
+        pltpu.VMEM((8, half, packed), bf16),
+        pltpu.VMEM((3, rows, packed), bf16),
+    ]
+
+
+def mixture(
+    row_pack, cot_all, expert_in, shared_win, expert_out, shared_wout, select, spots, residual
+):
+    rows, packed = row_pack.shape
+    width = packed - EXTRA
+    total_rows = cot_all.shape[0]
+    owned, part = expert_out.shape[0], expert_out.shape[1]
+    shared_part = shared_wout.shape[0]
+    seq = total_rows // lax.axis_size(EXPERT)
+    padded = select.shape[1]
+    bf16, f32 = jnp.bfloat16, jnp.float32
+    vmem = pl.BlockSpec(memory_space=pltpu.VMEM)
+    anywhere = pl.BlockSpec(memory_space=pl.ANY)
+    copies = GATHER_COPIES + 2 * SUM_COPIES
+    return pl.pallas_call(
+        functools.partial(
+            mixture_kernel, (rows, seq, width, owned, part, shared_part, padded)
+        ),
+        out_shape=(
+            jax.ShapeDtypeStruct((rows, width), bf16),
+            jax.ShapeDtypeStruct((rows, packed), f32),
+            jax.ShapeDtypeStruct((total_rows, packed), bf16),
+            jax.ShapeDtypeStruct((total_rows, 3 * padded), bf16),
+        ),
+        in_specs=[anywhere] * 6 + [vmem] * 3,
+        out_specs=(vmem,) * 2 + (anywhere,) * 2,
+        scratch_shapes=[
+            pltpu.VMEM((2 * padded, width), bf16),
+            pltpu.VMEM((padded, width), bf16),
+            pltpu.VMEM((seq, packed), bf16),
+            pltpu.VMEM((seq, width), bf16),
+            pltpu.VMEM((seq, 3 * padded), bf16),
+            pltpu.VMEM((seq, EXTRA), f32),
+            pltpu.VMEM((seq, width), bf16),
+            pltpu.VMEM((seq, packed), bf16),
+        ]
+        + sum_slots(rows, width)
+        + sum_slots(rows, packed)
+        + [
+            pltpu.SemaphoreType.DMA((copies,)),
+            pltpu.SemaphoreType.DMA((copies,)),
+            pltpu.SemaphoreType.DMA((2 * owned + 4,)),
+            pltpu.SemaphoreType.DMA((4,)),
+        ],
+        compiler_params=pltpu.CompilerParams(
+            collective_id=0, has_side_effects=True, vmem_limit_bytes=63 * 2**20
+        ),
+        cost_estimate=pl.CostEstimate(
+            flops=2 * total_rows * width * padded * 6,
+            bytes_accessed=100 * 2**20,
+            transcendentals=total_rows * padded,
+        ),
+        name="mixture",
+    )(
+        row_pack,
+        cot_all,
+        expert_in.transpose(0, 2, 3, 1).reshape(2 * owned * part, width),
+        shared_win,
+        expert_out.reshape(owned * part, width),
+        shared_wout,
+        select,
+        spots,
+        residual,
+    )
+
+
+class Totals:
+    def __init__(self, place, copies, value, from_c, from_y, from_x, by_z):
+        self.place, self.copies, self.value = place, copies, value
+        self.slots = {CORE: from_c, ROW: from_y, COLUMN: from_x}
+        self.by_z = by_z
+
+    def send(self, axis):
+        self.copies.start((TOTAL, axis), self.value, self.slots[axis], **{axis: 1})
+
+    def add(self, axis):
+        self.copies.arrived((TOTAL, axis))
+        self.copies.sent((TOTAL, axis))
+        self.value[...] = self.value[...] + self.slots[axis][...]
+
+    def send_z(self):
+        mine = self.by_z.at[self.place.z]
+        mine[...] = self.value[...]
+        for kz in (1, 2, 3):
+            self.copies.start(("tz", kz), mine, mine, kz=kz)
+
+    def finish(self):
+        for kz in (1, 2, 3):
+            self.copies.arrived(("tz", kz))
+        by_z = self.by_z
+        return (by_z[0] + by_z[1]) + (by_z[2] + by_z[3])
+
+
+class OwnerSums:
+    def __init__(self, place, copies, sources, mine, from_x, from_z, sems):
+        self.place, self.copies, self.sources = place, copies, sources
+        self.mine, self.from_x, self.from_z, self.sems = mine, from_x, from_z, sems
+
+    def view(self, i, kz, kx):
+        width = self.mine[i].shape[-2] if i == 0 else self.mine[i].shape[-1]
+        at = pl.ds(pl.multiple_of(self.place.sequence(kz, kx) * width, width), width)
+        return self.sources[i].at[:, at]
+
+    def begin(self, kz):
+        for i in (0, 1):
+            self.copies.start(("ox", i, kz), self.view(i, kz, 1), self.from_x[i].at[kz], kx=1)
+
+    def load(self, kz):
+        return [
+            pltpu.make_async_copy(
+                self.view(i, kz, 0), self.mine[i].at[kz % 2], self.sems.at[2 * (kz % 2) + i]
+            )
+            for i in (0, 1)
+        ]
+
+    def add(self, kz):
+        for load in self.load(kz):
+            load.wait()
+        for i in (0, 1):
+            self.copies.arrived(("ox", i, kz))
+            held = self.from_x[i].at[kz]
+            held[...] = held[...] + self.mine[i][kz % 2]
+            if kz:
+                self.copies.start(("oz", i, kz), held, self.from_z[i].at[kz - 1], kz=kz)
+
+    def finish(self, i, out_ref):
+        total = self.from_x[i][0].astype(jnp.float32)
+        for kz in (1, 2, 3):
+            self.copies.arrived(("oz", i, kz))
+            total = total + self.from_z[i][kz - 1].astype(jnp.float32)
+        out_ref[...] = total
+
+
+CLOSING_COPIES = 14 + 14 + 6
+
+
+def closing_kernel(
+    sizes,
+    rows_ref,
+    cot_ref,
+    units_ref,
+    att_in_ref,
+    att_out_ref,
+    small_ref,
+    att_in_out,
+    att_out_out,
+    small_out,
+    expert_in_out,
+    expert_out_out,
+    shared_in_out,
+    shared_out_out,
+    chunks,
+    turned,
+    columns,
+    grads,
+    shared_in_send,
+    shared_out_send,
+    own_in,
+    own_out,
+    in_x,
+    out_x,
+    in_z,
+    out_z,
+    small,
+    small_c,
+    small_y,
+    small_x,
+    small_z,
+    send_sems,
+    recv_sems,
+    own_sems,
+    chunk_sems,
+    column_sems,
+    write_sems,
+    keep_sems,
+):
+    width, owned, part, shared_part, owner_width, padded = sizes
+    f32, bf16 = jnp.float32, jnp.bfloat16
+    place = Place()
+    copies = Copies(place, send_sems, recv_sems)
+    totals = Totals(place, copies, small, small_c, small_y, small_x, small_z)
+    owners = OwnerSums(
+        place,
+        copies,
+        (att_in_ref, att_out_ref),
+        (own_in, own_out),
+        (in_x, out_x),
+        (in_z, out_z),
+        own_sems,
+    )
+    wide = 2 * owner_width
+    cut = owned * part
+    lanes = 128
+    per_kind = padded // lanes
+
+    def chunk_load(i, slot):
+        at = pl.ds(pl.multiple_of(i * lanes, lanes), lanes)
+        return pltpu.make_async_copy(
+            units_ref.at[:, at], chunks.at[slot], chunk_sems.at[slot]
+        )
+
+    def column_load(kz, which):
+        source = (rows_ref, cot_ref)[which]
+        at = pl.ds(pl.multiple_of(place.z_of(kz) * wide, wide), wide)
+        return pltpu.make_async_copy(source.at[:, at], columns.at[which], column_sems.at[which])
+
+    chunk_load(0, 0).start()
+    for load in owners.load(3) + owners.load(2):
+        load.start()
+    small[...] = small_ref[...]
+    greet(place, PARTNERS + FARTHER)
+    totals.send(CORE)
+    owners.begin(3)
+    owners.begin(2)
+    column_load(3, 0).start()
+    column_load(3, 1).start()
+
+    def turn(kind):
+        @pl.loop(kind * per_kind, (kind + 1) * per_kind)
+        def _(i):
+            slot = i % 2
+            chunk_load(i, slot).wait()
+
+            @pl.when(i + 1 < 3 * per_kind)
+            def _():
+                chunk_load(i + 1, 1 - slot).start()
+
+            to = pl.ds(pl.multiple_of(i * lanes, lanes), lanes)
+
+            @pl.loop(0, turned.shape[1] // wide)
+            def _(r):
+                at = pl.ds(pl.multiple_of(r * wide, wide), wide)
+                turned[to, at] = chunks[slot, at, :].T
+
+    def owners_add(kz):
+        owners.add(kz)
+        if kz >= 2:
+            for load in owners.load(kz - 2):
+                load.start()
+            owners.begin(kz - 2)
+
+    def span(kz):
+        return pl.ds(pl.multiple_of(place.z_of(kz) * wide, wide), wide)
+
+    def writes(kz, kind):
+        found = []
+        for e in range(owned):
+            if kind < 2:
+                target = expert_in_out.at[pl.ds((2 * e + kind) * part, part), span(kz)]
+            else:
+                target = expert_out_out.at[pl.ds(e * part, part), span(kz)]
+            found.append(
+                pltpu.make_async_copy(
+                    grads.at[kind, pl.ds(e * part, part)], target, write_sems.at[kind * owned + e]
+                )
+            )
+        return found
+
+    def share(kz, which):
+        sent = (shared_in_send, shared_out_send)[which]
+        target = (shared_in_out, shared_out_out)[which].at[place.sequence(0, 0)]
+        for kx in (1, 0):
+            at = pl.ds(pl.multiple_of(place.x_of(kx) * owner_width, owner_width), owner_width)
+            source = sent.at[kz, :, at]
+            if kz or kx:
+                copies.start((SHARE, which, kz, kx), source, target, kz=kz, kx=kx)
+            else:
+                pltpu.make_async_copy(source, target, keep_sems.at[which]).start()
+
+    def product(kz, kind):
+        which = kind // 2
+        if kind != 1:
+            column_load(kz, which).wait()
+        if kz < 3:
+            for write in writes(kz + 1, kind):
+                write.wait()
+
+        @pl.loop(0, 2)
+        def _(n):
+            at = pl.ds(pl.multiple_of(n * owner_width, owner_width), owner_width)
+            grads[kind, :, at] = jnp.dot(
+                turned[pl.ds(kind * padded, padded), :],
+                columns[which, :, at],
+                preferred_element_type=f32,
+            ).astype(bf16)
+
+        if kz and kind:
+            column_load(kz - 1, which).start()
+        for write in writes(kz, kind):
+            write.start()
+        shared = grads[kind, pl.ds(cut, shared_part), :]
+        if kind < 2:
+            shared_in_send[kz, pl.ds(kind * shared_part, shared_part), :] = shared
+        else:
+            shared_out_send[kz] = shared
+        if kind:
+            share(kz, which)
+
+    turn(0)
+    totals.add(CORE)
+    totals.send(ROW)
+    turn(1)
+    owners_add(3)
+    turn(2)
+    totals.add(ROW)
+    totals.send(COLUMN)
+    product(3, 0)
+    product(3, 1)
+    owners_add(2)
+    product(3, 2)
+    totals.add(COLUMN)
+    totals.send_z()
+    product(2, 0)
+    product(2, 1)
+    product(2, 2)
+    owners_add(1)
+    product(1, 0)
+    product(1, 1)
+    product(1, 2)
+    owners_add(0)
+    product(0, 0)
+    product(0, 1)
+    product(0, 2)
+    small_out[...] = totals.finish()
+    owners.finish(0, att_in_out)
+    owners.finish(1, att_out_out)
+    for kind in (0, 1, 2):
+        for write in writes(0, kind):
+            write.wait()
+    for which in (0, 1):
+        sent = (shared_in_send, shared_out_send)[which]
+        target = (shared_in_out, shared_out_out)[which].at[place.sequence(0, 0)]
+        at = pl.ds(pl.multiple_of(place.x_of(0) * owner_width, owner_width), owner_width)
+        pltpu.make_async_copy(sent.at[0, :, at], target, keep_sems.at[which]).wait()
+    for name in copies.made:
+        if name[0] == SHARE:
+            copies.arrived(name)
+    for name in copies.made:
+        if name[0] != TOTAL:
+            copies.sent(name)
+
+
+def closing(rows_all, cot_all, units_all, att_in, att_out, small, owned, part, shared_part):
+    total_rows, width = cot_all.shape
+    padded = units_all.shape[1] // 3
+    owners = lax.axis_size(EXPERT)
+    owner_width = width // owners
+    wide = 2 * owner_width
+    heads_width = att_in.shape[2]
+    bf16, f32 = jnp.bfloat16, jnp.float32
+    vmem = pl.BlockSpec(memory_space=pltpu.VMEM)
+    anywhere = pl.BlockSpec(memory_space=pl.ANY)
+    block_in = (3, owner_width, heads_width)
+    block_out = (heads_width, owner_width)
+    return pl.pallas_call(
+        functools.partial(
+            closing_kernel, (width, owned, part, shared_part, owner_width, padded)
+        ),
+        out_shape=(
+            jax.ShapeDtypeStruct(block_in, f32),
+            jax.ShapeDtypeStruct(block_out, f32),
+            jax.ShapeDtypeStruct(small.shape, f32),
+            jax.ShapeDtypeStruct((2 * owned * part, width), bf16),
+            jax.ShapeDtypeStruct((owned * part, width), bf16),
+            jax.ShapeDtypeStruct((owners, 2 * shared_part, owner_width), bf16),
+            jax.ShapeDtypeStruct((owners, shared_part, owner_width), bf16),
+        ),
+        in_specs=[anywhere] * 5 + [vmem],
+        out_specs=(vmem,) * 3 + (anywhere,) * 4,
+        scratch_shapes=[
+            pltpu.VMEM((2, total_rows, 128), bf16),
+            pltpu.VMEM((3 * padded, total_rows), bf16),
+            pltpu.VMEM((2, total_rows, wide), bf16),
+            pltpu.VMEM((3, padded, wide), bf16),
+            pltpu.VMEM((4, 2 * shared_part, wide), bf16),
+            pltpu.VMEM((4, shared_part, wide), bf16),
+            pltpu.VMEM((2,) + block_in, bf16),
+            pltpu.VMEM((2,) + block_out, bf16),
+            pltpu.VMEM((4,) + block_in, bf16),
+            pltpu.VMEM((4,) + block_out, bf16),
+            pltpu.VMEM((3,) + block_in, bf16),
+            pltpu.VMEM((3,) + block_out, bf16),
+        ]
+        + [pltpu.VMEM(small.shape, f32)] * 4
+        + [
+            pltpu.VMEM((4,) + small.shape, f32),
+            pltpu.SemaphoreType.DMA((CLOSING_COPIES,)),
+            pltpu.SemaphoreType.DMA((CLOSING_COPIES,)),
+            pltpu.SemaphoreType.DMA((4,)),
+            pltpu.SemaphoreType.DMA((2,)),
+            pltpu.SemaphoreType.DMA((2,)),
+            pltpu.SemaphoreType.DMA((3 * owned,)),
+            pltpu.SemaphoreType.DMA((2,)),
+        ],
+        compiler_params=pltpu.CompilerParams(
+            collective_id=1, has_side_effects=True, vmem_limit_bytes=62 * 2**20
+        ),
+        cost_estimate=pl.CostEstimate(
+            flops=2 * total_rows * width * padded * 3,
+            bytes_accessed=150 * 2**20,
+            transcendentals=0,
+        ),
+        name="closing",
+    )(rows_all, cot_all, units_all, att_in, att_out, small)
+
+
+OPENING_COPIES = 6 + 8 + 3 + 14
+
+
+def opening_kernel(
+    sizes,
+    normed_ref,
+    att_in_ref,
+    att_out_ref,
+    shared_in_ref,
+    shared_out_ref,
+    normed_all,
+    att_in_all,
+    att_out_all,
+    shared_in_all,
+    shared_out_all,
+    send_sems,
+    recv_sems,
+    own_sems,
+):
+    rows, owner_width, shared_part = sizes
+    place = Place()
+    copies = Copies(place, send_sems, recv_sems)
+
+    def in_view(kz, kx):
+        at = pl.ds(pl.multiple_of(place.sequence(kz, kx) * owner_width, owner_width), owner_width)
+        return att_in_all.at[:, at]
+
+    def out_view(kz, kx):
+        return att_out_all.at[place.sequence(kz, kx)]
+
+    here = pl.ds(
+        pl.multiple_of(place.sequence(0, 0) * owner_width, owner_width), owner_width
+    )
+    spot = pl.ds(pl.multiple_of((place.y * 2 + place.c) * rows, rows), rows)
+
+    def shared_block(kz, kx):
+        owner = place.sequence(kz, kx)
+        at = pl.ds(pl.multiple_of(owner * shared_part, shared_part), shared_part)
+        return (
+            (shared_in_ref.at[owner], shared_in_all.at[:, here]),
+            (shared_out_ref.at[at], shared_out_all.at[:, here]),
+        )
+
+    keeps = [
+        (normed_ref, normed_all.at[spot]),
+        (att_in_ref, in_view(0, 0)),
+        (att_out_ref, out_view(0, 0)),
+    ] + list(shared_block(0, 0))
+    keeps = [
+        pltpu.make_async_copy(source, target, own_sems.at[i])
+        for i, (source, target) in enumerate(keeps)
+    ]
+    for keep in keeps:
+        keep.start()
+    greet(place, PARTNERS + FARTHER + [dict(ky=1, kc=1)])
+
+    def spread_z(kz):
+        copies.start(("zi", kz), att_in_ref, in_view(0, 0), kz=kz)
+        copies.start(("zo", kz), att_out_ref, out_view(0, 0), kz=kz)
+
+    def pass_x(kz):
+        if kz:
+            copies.arrived(("zi", kz))
+        source = in_view(kz, 0) if kz else att_in_ref
+        copies.start(("xi", kz), source, in_view(kz, 0), kx=1)
+        if kz:
+            copies.arrived(("zo", kz))
+        source = out_view(kz, 0) if kz else att_out_ref
+        copies.start(("xo", kz), source, out_view(kz, 0), kx=1)
+
+    def share(kz, kx):
+        for which, (source, target) in enumerate(shared_block(kz, kx)):
+            copies.start((SHARE, which, kz, kx), source, target, kz=kz, kx=kx)
+
+    spread_z(1)
+    pass_x(0)
+    spread_z(2)
+    for ky, kc in ((0, 1), (1, 0), (1, 1)):
+        copies.start(("n", ky, kc), normed_ref, normed_all.at[spot], ky=ky, kc=kc)
+    pass_x(1)
+    spread_z(3)
+    pass_x(2)
+    share(1, 0)
+    share(1, 1)
+    pass_x(3)
+    share(3, 0)
+    share(3, 1)
+    share(2, 0)
+    share(2, 1)
+    share(0, 1)
+    for keep in keeps:
+        keep.wait()
+    for name in copies.made:
+        if name[0] not in ("zi", "zo") :
+            copies.arrived(name)
+    for name in copies.made:
+        copies.sent(name)
+
+
+def opening(normed, att_in, att_out, shared_in, shared_out):
+    rows, width = normed.shape
+    parts, owner_width, heads_width = att_in.shape
+    owners = lax.axis_size(EXPERT)
+    shards = lax.axis_size(SHARD)
+    shared_part = shared_out.shape[0] // owners
+    anywhere = pl.BlockSpec(memory_space=pl.ANY)
+    bf16 = jnp.bfloat16
+    return pl.pallas_call(
+        functools.partial(opening_kernel, (rows, owner_width, shared_part)),
+        out_shape=(
+            jax.ShapeDtypeStruct((rows * shards, width), bf16),
+            jax.ShapeDtypeStruct((parts, owner_width * owners, heads_width), bf16),
+            jax.ShapeDtypeStruct((owners,) + att_out.shape, bf16),
+            jax.ShapeDtypeStruct((2 * shared_part, width), bf16),
+            jax.ShapeDtypeStruct((shared_part, width), bf16),
+        ),
+        in_specs=[anywhere] * 5,
+        out_specs=(anywhere,) * 5,
+        scratch_shapes=[
+            pltpu.SemaphoreType.DMA((OPENING_COPIES,)),
+            pltpu.SemaphoreType.DMA((OPENING_COPIES,)),
+            pltpu.SemaphoreType.DMA((5,)),
+        ],
+        compiler_params=pltpu.CompilerParams(
+            collective_id=2, has_side_effects=True, vmem_limit_bytes=62 * 2**20
+        ),
+        cost_estimate=pl.CostEstimate(
+            flops=10**11, bytes_accessed=600 * 2**20, transcendentals=0
+        ),
+        name="opening",
+    )(normed, att_in, att_out, shared_in, shared_out)
+
+
+def attention_forward(queries, keys_all, values, score_scale):
+    scores = block_scores(queries, keys_all, 0, score_scale)
+    highest = jnp.max(scores, axis=-1, keepdims=True)
+    raised = jnp.exp(scores - highest)
+    probs = raised / jnp.sum(raised, axis=-1, keepdims=True)
+    mixed_out = jnp.einsum(
+        "hqk,khd->qhd", probs.astype(jnp.bfloat16), values, preferred_element_type=jnp.float32
+    )
+    return mixed_out, probs
+
+
+def attention_backward(queries, keys_all, values, probs, grad_out, score_scale):
+    value_grad = jnp.einsum(
+        "hqk,qhd->khd", probs.astype(jnp.bfloat16), grad_out, preferred_element_type=jnp.float32
+    )
+    prob_grad = jnp.einsum("qhd,khd->hqk", grad_out, values, preferred_element_type=jnp.float32)
+    score_grad = (
+        probs * (prob_grad - jnp.sum(prob_grad * probs, axis=-1, keepdims=True))
+    ).astype(jnp.bfloat16)
+    query_grad = jnp.einsum(
+        "hqk,khd->qhd", score_grad, keys_all, preferred_element_type=jnp.float32
+    )
+    key_grad = jnp.einsum("hqk,qhd->khd", score_grad, queries, preferred_element_type=jnp.float32)
+    return query_grad * score_scale, key_grad * score_scale, value_grad
+
+
+def local_gather(
+    tokens,
+    first_gain,
+    attention_in,
+    attention_bias,
+    attention_out,
+    second_gain,
+    router,
+    shared_gate,
+    shared_in,
+    shared_out,
+    expert_in,
+    expert_out,
+    cotangent,
+    expert_picks,
+):
+    bf16, f32 = jnp.bfloat16, jnp.float32
+    axes = (EXPERT, SHARD)
+    local_rows, width = tokens.shape
+    shards = lax.axis_size(SHARD)
+    owners = lax.axis_size(EXPERT)
+    owner = lax.axis_index(EXPERT)
+    seq_length = local_rows * shards
+    experts = router.shape[1]
+    owned = expert_in.shape[0]
+    part = expert_in.shape[3]
+    heads_here = attention_bias.shape[1]
+    head_dim = attention_bias.shape[2] * owners
+    score_scale = head_dim ** (-0.5)
+    shared_part = shared_in.shape[2] // owners
+    slice_rows = width // owners
+    cosine_table, sine_table = rope_tables(seq_length, head_dim)
+
+    inputs = tokens.astype(f32)
+    first_norm, first_factor = normalize(inputs)
+    first_low = (first_norm * first_gain).astype(bf16)
+    small = jnp.concatenate(
+        [router.reshape(-1), shared_gate, attention_bias.reshape(-1)]
+    )
+    small_rows = -(-small.shape[0] // slice_rows)
+    small_rows = -(-small_rows // 16) * 16
+    small = jnp.pad(small, (0, small_rows * slice_rows - small.shape[0]))
+    small = small.reshape(small_rows, slice_rows)
+    shared_blocks = shared_in.transpose(1, 2, 0).reshape(2, owners, shared_part, slice_rows)
+    shared_blocks = shared_blocks.transpose(1, 0, 2, 3).reshape(owners, -1, slice_rows)
+    cot_all = lax.all_gather(cotangent, axes, axis=0, tiled=True)
+    normed_all, att_in, out_small, shared_win, shared_wout = opening(
+        first_low,
+        attention_in.transpose(1, 0, 2),
+        jnp.concatenate([attention_out, small], axis=0),
+        shared_blocks,
+        shared_out,
+    )
+    normed_all, att_in, cot_all = lax.optimization_barrier((normed_all, att_in, cot_all))
+    att_out = out_small[:, : attention_out.shape[0]].transpose(1, 0, 2)
+    att_out = att_out.reshape(attention_out.shape[0], width)
+    small_all = out_small[:, attention_out.shape[0] :].reshape(owners, -1)
+    router_size = router.size
+    router_full = small_all[:, :router_size].reshape(width, experts)
+    gate_full = small_all[:, router_size : router_size + slice_rows].reshape(width)
+    bias_start = router_size + slice_rows
+    att_bias = small_all[:, bias_start : bias_start + attention_bias.size]
+    att_bias = att_bias.reshape((owners,) + attention_bias.shape).transpose(1, 2, 0, 3)
+    att_bias = att_bias.reshape(3, heads_here * head_dim)
+
+    projected = jnp.einsum("sd,cdf->scf", normed_all, att_in, preferred_element_type=f32)
+    projected = projected + att_bias.astype(f32)[None]
+    projected = projected.reshape(seq_length, 3, heads_here, head_dim)
+    queries = rotate(projected[:, 0], cosine_table, sine_table).astype(bf16)
+    keys_all = rotate(projected[:, 1], cosine_table, sine_table).astype(bf16)
+    values = projected[:, 2].astype(bf16)
+    attended, probs = attention_forward(queries, keys_all, values, score_scale)
+    attended_low = attended.astype(bf16).reshape(seq_length, -1)
+    attn_part = jnp.dot(attended_low, att_out, preferred_element_type=f32)
+    attn_local = lax.psum_scatter(
+        attn_part.astype(bf16), SHARD, scatter_dimension=0, tiled=True
+    ).astype(f32)
+    residual = inputs + attn_local
+    second_norm, second_factor = normalize(residual)
+    second_low = (second_norm * second_gain).astype(bf16)
+    logits = jnp.dot(second_low, router_full, preferred_element_type=f32)
+    route_probs = jax.nn.softmax(logits, axis=-1)
+    picked = jnp.sum(
+        (
+            expert_picks[:, :, None] == jnp.arange(experts, dtype=jnp.int32)[None, None, :]
+        ).astype(f32),
+        axis=1,
+    )
+    shared_scale = jax.nn.sigmoid(jnp.dot(second_low, gate_full, preferred_element_type=f32))
+
+    weights_here = jnp.concatenate([picked * route_probs, shared_scale[:, None]], axis=1)
+    coarse = weights_here.astype(bf16)
+    fine = (weights_here - coarse.astype(f32)).astype(bf16)
+    filler = jnp.zeros((local_rows, EXTRA - 2 * (experts + 1)), bf16)
+    row_pack = jnp.concatenate([second_low, coarse, fine, filler], axis=1)
+    units = owned * part + shared_part
+    padded = -(-units // 128) * 128
+    unit = jnp.arange(padded)
+    column = jnp.where(unit < owned * part, owner * owned + unit // part, experts)
+    column = jnp.where(unit < units, column, -1)
+    kinds = jnp.arange(EXTRA)
+    spots = (kinds[None, :] == column[:, None]).astype(bf16)
+    finer = jnp.where(unit < units, column + experts + 1, -1)
+    select = (kinds[:, None] == column[None, :]) | (kinds[:, None] == finer[None, :])
+    output, back_local, rows_all, units_all = mixture(
+        row_pack,
+        cot_all,
+        expert_in,
+        shared_win,
+        expert_out,
+        shared_wout,
+        select.astype(bf16),
+        spots,
+        residual,
+    )
+    first_dims = (((0,), (0,)), ((), ()))
+    out_grad = cotangent.astype(f32)
+    pick_grads = back_local[:, width : width + experts] * picked
+    logit_grad = (
+        route_probs
+        * (pick_grads - jnp.sum(pick_grads * route_probs, axis=-1, keepdims=True))
+    ).astype(bf16)
+    gate_logit_grad = (
+        back_local[:, width + experts] * shared_scale * (1.0 - shared_scale)
+    ).astype(bf16)
+    local_back = lax.dot_general(
+        logit_grad, router_full, (((1,), (1,)), ((), ())), preferred_element_type=f32
+    )
+    local_back = local_back + gate_logit_grad.astype(f32)[:, None] * gate_full.astype(f32)[None]
+    second_grad = local_back + back_local[:, :width]
+    residual_back, second_gain_grad = norm_back(
+        second_grad, second_norm, second_factor, second_gain
+    )
+    residual_grad = out_grad + residual_back
+    residual_all = lax.all_gather(residual_grad.astype(bf16), SHARD, axis=0, tiled=True)
+    att_out_grad = lax.dot_general(
+        attended_low, residual_all, first_dims, preferred_element_type=f32
+    )
+    attended_grad = lax.dot_general(
+        residual_all, att_out, (((1,), (1,)), ((), ())), preferred_element_type=f32
+    )
+    attended_grad = attended_grad.astype(bf16).reshape(seq_length, heads_here, head_dim)
+    query_grad, key_grad, value_grad = attention_backward(
+        queries, keys_all, values, probs, attended_grad, score_scale
+    )
+    projected_grad = jnp.stack(
+        [
+            rotate_back(query_grad, cosine_table, sine_table),
+            rotate_back(key_grad, cosine_table, sine_table),
+            value_grad,
+        ],
+        axis=1,
+    )
+    projected_grad = projected_grad.astype(bf16).reshape(seq_length, 3, heads_here * head_dim)
+    att_in_grad = jnp.einsum("sd,scf->cdf", normed_all, projected_grad, preferred_element_type=f32)
+    att_bias_grad = jnp.sum(projected_grad.astype(f32), axis=0)
+    first_part = jnp.einsum("scf,cdf->sd", projected_grad, att_in, preferred_element_type=f32)
+    first_grad = lax.psum_scatter(
+        first_part.astype(bf16), SHARD, scatter_dimension=0, tiled=True
+    ).astype(f32)
+    input_back, first_gain_grad = norm_back(first_grad, first_norm, first_factor, first_gain)
+    input_grad = residual_grad + input_back
+
+    vec_grads = jnp.concatenate([logit_grad, gate_logit_grad[:, None]], axis=1)
+    vec_grads = lax.dot_general(vec_grads, second_low, first_dims, preferred_element_type=f32)
+    bias_wide = jnp.zeros((3, shards, heads_here * head_dim), f32)
+    bias_wide = lax.dynamic_update_slice_in_dim(
+        bias_wide, att_bias_grad[:, None], lax.axis_index(SHARD), 1
+    )
+    bias_rows = bias_wide.size // width
+    first_bias = experts + 3
+    small = jnp.concatenate(
+        [vec_grads, second_gain_grad[None], first_gain_grad[None], bias_wide.reshape(-1, width)]
+    )
+    small = jnp.pad(small, ((0, -small.shape[0] % 8), (0, 0)))
+    (
+        att_in_local,
+        att_out_local,
+        summed,
+        expert_in_grad,
+        expert_out_grad,
+        shared_in_local,
+        shared_out_local,
+    ) = closing(
+        rows_all,
+        cot_all,
+        units_all,
+        att_in_grad.astype(bf16),
+        att_out_grad.astype(bf16),
+        small,
+        owned,
+        part,
+        shared_part,
+    )
+    expert_in_grad = expert_in_grad.reshape(owned, 2, part, width).transpose(0, 3, 1, 2)
+    expert_in_grad = expert_in_grad.astype(f32)
+    expert_out_grad = expert_out_grad.reshape(owned, part, width).astype(f32)
+    shared_in_local = shared_in_local.reshape(owners, 2, shared_part, slice_rows)
+    shared_in_local = shared_in_local.transpose(3, 1, 0, 2).reshape(slice_rows, 2, -1).astype(f32)
+    shared_out_local = shared_out_local.reshape(-1, slice_rows).astype(f32)
+    vec_local = lax.dynamic_slice_in_dim(
+        summed[: experts + 1], owner * slice_rows, slice_rows, axis=1
+    )
+    bias_all = summed[first_bias : first_bias + bias_rows].reshape(
+        3, shards, heads_here, owners, head_dim // owners
+    )
+    att_bias_local = lax.dynamic_index_in_dim(bias_all, lax.axis_index(SHARD), 1, False)
+    att_bias_local = lax.dynamic_index_in_dim(att_bias_local, owner, 2, False)
+    return (
+        output,
+        input_grad,
+        summed[experts + 2],
+        att_in_local.transpose(1, 0, 2),
+        att_bias_local,
+        att_out_local,
+        summed[experts + 1],
+        vec_local[:experts].T,
+        vec_local[experts],
+        shared_in_local,
+        shared_out_local,
+        expert_in_grad,
+        expert_out_grad,
+    )
+
+
 def solution(mesh):
     in_specs = (
-        P(("expert", "shard"), None),
+        P((EXPERT, SHARD), None),
         P(),
-        P("expert", None, "shard"),
-        P(None, "shard", "expert"),
-        P("shard", "expert"),
+        P(EXPERT, None, SHARD),
+        P(None, SHARD, EXPERT),
+        P(SHARD, EXPERT),
         P(),
-        P("expert", None),
-        P("expert"),
-        P("expert", None, "shard"),
-        P("shard", "expert"),
-        P("expert", None, None, "shard"),
-        P("expert", "shard", None),
-        P(("expert", "shard"), None),
-        P(("expert", "shard"), None),
+        P(EXPERT, None),
+        P(EXPERT),
+        P(EXPERT, None, SHARD),
+        P(SHARD, EXPERT),
+        P(EXPERT, None, None, SHARD),
+        P(EXPERT, SHARD, None),
+        P((EXPERT, SHARD), None),
+        P((EXPERT, SHARD), None),
     )
     out_specs = (
-        P(("expert", "shard"), None),
-        P(("expert", "shard"), None),
+        P((EXPERT, SHARD), None),
+        P((EXPERT, SHARD), None),
         P(),
-        P("expert", None, "shard"),
-        P(None, "shard", "expert"),
-        P("shard", "expert"),
+        P(EXPERT, None, SHARD),
+        P(None, SHARD, EXPERT),
+        P(SHARD, EXPERT),
         P(),
-        P("expert", None),
-        P("expert"),
-        P("expert", None, "shard"),
-        P("shard", "expert"),
-        P("expert", None, None, "shard"),
-        P("expert", "shard", None),
-    )
-    return jax.shard_map(local, mesh=mesh, in_specs=in_specs, out_specs=out_specs, check_vma=False)
+        P(EXPERT, None),
+        P(EXPERT),
+        P(EXPERT, None, SHARD),
+        P(SHARD, EXPERT),
+        P(EXPERT, None, None, SHARD),
+        P(EXPERT, SHARD, None),
+    )
+    plan = local_gather if mesh.size <= 32 else local_exchange
+    return jax.shard_map(plan, mesh=mesh, in_specs=in_specs, out_specs=out_specs, check_vma=False)

time: 2100 us -> 936 us (0.45)
  waiting for transfers between devices: 1390 us -> 90.7 us
  Pallas kernels: 0 us -> 701 us
  blocking collectives: 292 us -> 0 us
  matrix products: 206 us -> 45.2 us
  local copies, waits for them, and re-layouts: 81.9 us -> 38.5 us
  other arithmetic: 76.5 us -> 36 us
  starting transfers between devices: 26.7 us -> 0.33 us
    pallas_call x0 -> x3, Pallas kernels: none -> 701 us  [the longest x1 295 us: mixture(): pl.pallas_call(functools.partial(mixture_kernel, (rows, seq, width, owned...]
    reduce_scatter x12 -> x2, waiting for transfers between devices: 721 us -> 47.2 us  [the longest x1 28.6 us: local_gather(): lax.psum_scatter(attn_part.astype(bf16), SHARD, scatter_dimension=0, tile...]
    all_gather x10 -> x2, waiting for transfers between devices: 553 us -> 42.8 us  [the longest x1 42.8 us: local_gather(): lax.all_gather(residual_grad.astype(bf16), SHARD, axis=0, tiled=True)]
    all_gather x5 -> x0, blocking collectives: 227 us -> none  [the longest x1 168 us: fetch_dense(): lax.all_gather(router, 'expert', axis=0, tiled=True)]
    dot_general x31 -> x15, matrix products: 206 us -> 41.5 us  [the longest x1 7.74 us: local_gather(): jnp.einsum('scf,cdf->sd', projected_grad, att_in, preferred_element_type=...]
    unnamed x24 -> x4, waiting for transfers between devices: 58 us -> 0.73 us
    all_to_all x4 -> x0, waiting for transfers between devices: 56.8 us -> none  [the longest x1 56.8 us: local(): lax.all_to_all(expert_result, 'expert', split_axis=0, concat_axis=0, tile...]
    psum x1 -> x0, blocking collectives: 43.7 us -> none  [local(): lax.psum((first_gain_grad, second_gain_grad), ('expert', 'shard'))]
  transfers between devices with their start and end apart: 27 -> 4, of which waited for: 20 -> 3; matrix products, arithmetic and copies ran while one was open for 16% -> 3% of each run, Pallas kernels for 0% -> 24%
where the time goes in v1:
time: 936 us; the launch traced here: 926 us
  Pallas kernels  701 us (75%)
  waiting for transfers between devices  90.7 us (10%)
  matrix products  45.2 us (5%)
  local copies, waits for them, and re-layouts  38.5 us (4%)
  other arithmetic  36 us (4%)
  between operations  14.9 us (2%)
    pallas_call x1, Pallas kernels, mixture(): pl.pallas_call(functools.partial(mixture_kernel, (rows, seq, width, owned...  295 us
    pallas_call x1, Pallas kernels, opening(): pl.pallas_call(functools.partial(opening_kernel, (rows, owner_width, shar...  225 us
    pallas_call x1, Pallas kernels, closing(): pl.pallas_call(functools.partial(closing_kernel, (width, owned, part, sha...  181 us
    all_gather x1, waiting for transfers between devices, local_gather(): lax.all_gather(residual_grad.astype(bf16), SHARD, axis=0, tiled=True)  42.8 us
    reduce_scatter x1, waiting for transfers between devices, local_gather(): lax.psum_scatter(attn_part.astype(bf16), SHARD, scatter_dimension=0, tile...  28.6 us
  transfers between devices with their start and end apart: 4, of which 3 were waited for; matrix products, arithmetic and copies ran while one was open for 3% of the time, Pallas kernels for 24%

profile of v1, /device:TPU:0, one launch (start us, length us, event | category | flops | bytes accessed | tf_op | source)
XLA Modules:
  0.0 926.3 jit_solution(5845818632159823943)
XLA Ops:
  8.0 3.7 copy.127
  11.7 1.2 copy.128
  14.3 1.0 fusion.23.normed_ref
  15.2 225.0 %opening.1 = (bf16[512,2048]{1,0:T(8,128)(2,1)}, bf16[3,2048,512]{2,1,0:T(8,128)(2,1)}, bf16[8,544,256]{2,1,0:T(8,128)(2,1)}, bf16[352,2048]{1,0:T(8,128)(2,1)}, bf16[176,2048]{1,0:T(8,128)(2,1)}) custom-call(bf16[128,2048]{1,0:T(8,128)(2,1)} %fusion.23.normed_ref, bf16[3,256,512]{2,1,0:T(8,128)(2,1)} %bitcast.166, ...), custom_call_target="tpu_custom_call" | custom-call | flops 99999997952 | bytes 629145600 | tf_op jit(solution)/shard_map/opening/pallas_call | solution.py:1419
  240.2 0.9 slice_bitcast_fusion.3
  241.4 1.7 slice_bitcast_fusion
  243.2 2.4 copy.134
  247.0 6.3 fusion.9
  253.8 1.2 copy-done.7
  255.6 3.7 fusion.72
  259.4 3.1 convolution_convert_fusion.4
  263.3 2.6 convolution_convert_fusion.1
  268.5 28.6 %reduce-scatter.3.cloned.1.call-done = bf16[128,2048]{1,0:T(8,128)(2,1)} async-done(((bf16[512,2048]{1,0:T(8,128)(2,1)}), bf16[128,2048]{1,0:T(8,128)(2,1)}) %reduce-scatter.3.cloned.1.call-update) | async-done | bytes 524304 | tf_op jit(solution)/shard_map/reduce_scatter | solution.py:1545
  297.0 2.2 convert_add_fusion
  300.8 1.1 concatenate.45.block_ref
  302.0 294.9 %mixture.1 = (bf16[128,2048]{1,0:T(8,128)(2,1)}, f32[128,2176]{1,0:T(8,128)}, bf16[4096,2176]{1,0:T(8,128)(2,1)}, bf16[4096,2688]{1,0:T(8,128)(2,1)}) custom-call(bf16[128,2176]{1,0:T(8,128)(2,1)} %concatenate.45.block_ref, bf16[4096,2048]{1,0:T(8,128)(2,1)} %all-gather.3.cloned.1.call-done.cot_ref, bf16[1408,2048]{1,0:T(8,128)(2,1)} %bitcast.164, ...), custom_call_target="tpu_custom_call" | custom-call | flops 90194313216 | bytes 104857600 | tf_op jit(solution)/shard_map/mixture/pallas_call | solution.py:920
  596.9 1.1 multiply_reduce_fusion.4
  598.0 1.0 slice_reduce_fusion
  599.0 1.0 multiply_convert_fusion.2
  600.0 2.2 multiply_reduce_fusion.1
  602.2 1.0 copy-done.5
  603.2 1.3 fusion.68
  604.7 42.8 %all-gather.5.cloned.1.call-done = bf16[512,2048]{1,0:T(8,128)(2,1)} async-done(((bf16[128,2048]{1,0:T(8,128)(2,1)}), bf16[512,2048]{1,0:T(8,128)(2,1)}) %all-gather.5.cloned.1.call-update) | async-done | bytes 2097168 | tf_op jit(solution)/shard_map/all_gather | solution.py:1605
  647.5 3.7 convolution_convert_fusion.2
  651.1 2.0 multiply_reduce_fusion
  653.2 1.6 convolution_convert_fusion.3
  654.8 1.2 multiply_convert_fusion
  658.6 1.4 fusion.31
  660.2 1.3 copy.146
  661.5 2.2 copy.147
  663.7 7.7 bitcast_convert_fusion
  671.5 0.9 copy-done.2
  672.7 1.4 convert_reduce_fusion
  674.3 4.5 convolution_convert_fusion.att_out_ref
  678.8 5.6 convert_bitcast_fusion.1.att_in_ref
  684.4 18.7 %reduce-scatter.5.cloned.1.call-done = bf16[128,2048]{1,0:T(8,128)(2,1)} async-done(((bf16[512,2048]{1,0:T(8,128)(2,1)}), bf16[128,2048]{1,0:T(8,128)(2,1)}) %reduce-scatter.5.cloned.1.call-update) | async-done | bytes 524304 | tf_op jit(solution)/shard_map/reduce_scatter | solution.py:1628
  703.1 1.5 fusion.25
  705.3 180.8 %closing.1 = (f32[3,256,512]{2,1,0:T(8,128)}, f32[512,256]{1,0:T(8,128)}, f32[24,2048]{1,0:T(8,128)}, bf16[1408,2048]{1,0:T(8,128)(2,1)}, bf16[704,2048]{1,0:T(8...) custom-call(bf16[4096,2176]{1,0:T(8,128)(2,1)} %get-tuple-element.42.rows_ref, ...), custom_call_target="tpu_custom_call" | custom-call | flops 45097156608 | bytes 157286400 | tf_op jit(solution)/shard_map/closing/pallas_call | solution.py:1260
  887.0 1.5 fusion.71
  888.5 8.8 convert_bitcast_fusion
  897.3 3.3 convert.33
  900.6 1.9 copy.151
  902.5 5.5 copy.152
  908.0 2.4 bitcast_convert_fusion.1
  910.5 1.3 dynamic-slice_bitcast_fusion
  911.9 1.3 dynamic-slice.3
  913.7 2.8 fusion.22
  917.4 1.1 copy.173
  (142 shorter events, 16.9 us)
Async XLA Ops:
  7.2 239.9 %all-gather.3.cloned.1.call-start = ((), (), s32[]{:S(2)}) async-start(), calls=%async_computation.2 | async-start | bytes 17301504 | tf_op jit(solution)/shard_map/all_gather | solution.py:1516
  7.9 289.1 %reduce-scatter.3.cloned.1.call-start = ((), (), s32[]{:S(2)}) async-start(), calls=%async_computation.3 | async-start | bytes 2621440 | tf_op jit(solution)/shard_map/reduce_scatter | solution.py:1545
  11.7 1.3 copy-start.29
  11.7 1.5 copy-start.32
  11.7 1.6 copy-start.34
  11.7 1.6 copy-start.25
  11.7 2.3 copy-start
  11.7 2.5 copy-start.27
  14.2 1.0 copy-start.30
  253.3 1.7 copy-start.7
  255.6 3.8 copy-start.16
  255.6 3.8 copy-start.18
  259.4 3.9 copy-start.15
  262.5 0.8 copy-start.35
  265.9 0.7 copy-start.33
  266.0 33.3 %copy-start.26 = (f32[2048]{0:T(1024)S(1)}, f32[2048]{0:T(1024)}, u32[]{:S(2)}) copy-start(f32[2048]{0:T(1024)} %param.19) | copy-start | bytes 24580
  266.0 381.5 %all-gather.5.cloned.1.call-start = ((), (), s32[]{:S(2)}) async-start(), calls=%async_computation.4 | async-start | bytes 2621440 | tf_op jit(solution)/shard_map/all_gather | solution.py:1605
  266.6 32.9 %copy-start.8 = (bf16[2048,16]{1,0:T(8,128)(2,1)}, bf16[2048,16]{1,0:T(8,128)(2,1)S(1)}, u32[]{:S(2)}) copy-start(bf16[2048,16]{1,0:T(8,128)(2,1)S(1)} %reshape.228) | copy-start | bytes 196612
  297.0 2.3 copy-start.3
  299.5 1.3 copy-start.1
  596.8 6.3 copy-start.4
  596.8 6.3 copy-start.9
  602.2 1.0 copy-start.5
  604.5 98.6 %reduce-scatter.5.cloned.1.call-start = ((), (), s32[]{:S(2)}) async-start(), calls=%async_computation.5 | async-start | bytes 2621440 | tf_op jit(solution)/shard_map/reduce_scatter | solution.py:1628
  647.5 3.7 copy-start.10
  654.8 1.2 copy-start.19
  656.0 1.0 copy-start.17
  657.6 1.0 copy-start.22
  661.4 2.3 copy-start.12
  671.4 1.0 copy-start.2
  674.2 4.5 copy-start.13
  674.2 4.5 copy-start.14
  674.3 4.5 copy-start.36
  678.8 24.3 %copy-start.28 = (f32[2048]{0:T(1024)S(1)}, f32[2048]{0:T(1024)}, u32[]{:S(2)}) copy-start(f32[2048]{0:T(1024)} %param.15) | copy-start | bytes 24580
  678.8 24.3 %copy-start.31 = (f32[128]{0:T(128)S(1)}, f32[128]{0:T(128)}, u32[]{:S(2)}) copy-start(f32[128]{0:T(128)} %copy-done.30) | copy-start | bytes 1540
  888.5 8.8 copy-start.11
  897.3 3.3 copy-start.21
  908.0 5.7 copy-start.6
  913.7 2.8 copy-start.23
  913.7 3.6 copy-start.20
  916.6 1.9 copy-start.24
Sparse Core Ops, SparseCore 0:
  10.9 217.8 all-gather.2
  266.1 30.8 reduce-scatter.2
  604.6 42.8 all-gather.4
  671.6 31.4 reduce-scatter.4

commit v2 on v1

--- a/solution.py
+++ b/solution.py
@@ -484,7 +484,7 @@
 class Copies:
     def __init__(self, place, send_sems, recv_sems):
         self.place, self.send_sems, self.recv_sems = place, send_sems, recv_sems
-        self.made = {}
+        self.made, self.got, self.left = {}, set(), set()
 
     def start(self, name, source, target, **partner):
         at = len(self.made)
@@ -500,10 +500,14 @@
         self.made[name] = copy
 
     def arrived(self, name):
-        self.made[name].wait_recv()
+        if name not in self.got:
+            self.got.add(name)
+            self.made[name].wait_recv()
 
     def sent(self, name):
-        self.made[name].wait_send()
+        if name not in self.left:
+            self.left.add(name)
+            self.made[name].wait_send()
 
 
 GATHER_COPIES = 55
@@ -642,9 +646,41 @@
         return total
 
 
+RAISE, OUT, BACK, CORES, BEGIN, PASS, PASS_X, PASS_Y, PASS_LAST, HAVE = range(10)
+FIRST, AWAY, HERE, THIRD = range(10, 14)
+ORDER = ((0, 1), (3, 1), (3, 0), (2, 1), (2, 0), (1, 1), (1, 0), (0, 0))
+PLAN = (
+    (PASS, 0, 0), (BEGIN, 1, 0), (BEGIN, 3, 0), (PASS_Y, 0, 0), (PASS_X, 0, 0),
+    (PASS_LAST, 0, 0), (PASS, 3, 0), (HAVE, 0, 0), (RAISE, 0, 0), (BEGIN, 2, 0), (RAISE, 0, 1),
+    (PASS_X, 3, 0), (PASS_Y, 3, 0), (RAISE, 0, 2), (RAISE, 0, 3), (PASS, 1, 0), (OUT, 0, 0),
+    (OUT, 0, 1), (CORES, 0, 0), (BACK, 0, 0), (PASS_LAST, 3, 0), (BACK, 0, 1), (CORES, 1, 0),
+    (HAVE, 1, 0), (PASS, 2, 0), (PASS_Y, 1, 0), (RAISE, 1, 0), (RAISE, 1, 1), (RAISE, 1, 2),
+    (PASS_Y, 2, 0), (RAISE, 1, 3), (HAVE, 2, 0), (FIRST, 0, 0), (OUT, 1, 0), (OUT, 1, 1),
+    (CORES, 0, 1), (FIRST, 1, 0), (BACK, 1, 0), (PASS_X, 2, 0), (BACK, 1, 1), (CORES, 1, 1),
+    (RAISE, 2, 0), (RAISE, 2, 1), (FIRST, 0, 1), (RAISE, 2, 2), (FIRST, 1, 1), (RAISE, 2, 3),
+    (OUT, 2, 0), (OUT, 2, 1), (CORES, 0, 2), (BACK, 2, 0), (BACK, 2, 1), (PASS_LAST, 2, 0),
+    (CORES, 1, 2), (AWAY, 0, 3), (HAVE, 3, 0), (FIRST, 1, 2), (FIRST, 0, 2), (RAISE, 3, 0),
+    (RAISE, 3, 1), (RAISE, 3, 2), (RAISE, 3, 3), (PASS_X, 1, 0), (OUT, 3, 0), (OUT, 3, 1),
+    (CORES, 0, 3), (BACK, 3, 0), (AWAY, 1, 3), (HAVE, 4, 0), (BACK, 3, 1), (CORES, 1, 3),
+    (HERE, 0, 3), (FIRST, 0, 3), (RAISE, 4, 0), (RAISE, 4, 1), (RAISE, 4, 2), (PASS_LAST, 1, 0),
+    (FIRST, 1, 3), (RAISE, 4, 3), (HAVE, 5, 0), (OUT, 4, 0), (THIRD, 0, 3), (AWAY, 0, 2),
+    (HERE, 1, 3), (OUT, 4, 1), (CORES, 0, 4), (BACK, 4, 0), (BACK, 4, 1), (FIRST, 0, 4),
+    (CORES, 1, 4), (RAISE, 5, 0), (RAISE, 5, 1), (RAISE, 5, 2), (RAISE, 5, 3), (FIRST, 1, 4),
+    (THIRD, 1, 3), (OUT, 5, 0), (OUT, 5, 1), (AWAY, 1, 2), (HERE, 0, 2), (CORES, 0, 5),
+    (BACK, 5, 0), (BACK, 5, 1), (CORES, 1, 5), (FIRST, 0, 5), (HAVE, 6, 0), (HERE, 1, 2),
+    (FIRST, 1, 5), (RAISE, 6, 0), (RAISE, 6, 1), (RAISE, 6, 2), (RAISE, 6, 3), (OUT, 6, 0),
+    (THIRD, 0, 2), (HAVE, 7, 0), (OUT, 6, 1), (CORES, 0, 6), (AWAY, 0, 1), (BACK, 6, 0),
+    (THIRD, 1, 2), (FIRST, 0, 6), (BACK, 6, 1), (CORES, 1, 6), (RAISE, 7, 0), (HERE, 0, 1),
+    (AWAY, 1, 1), (RAISE, 7, 1), (RAISE, 7, 2), (FIRST, 1, 6), (RAISE, 7, 3), (THIRD, 0, 1),
+    (OUT, 7, 0), (AWAY, 0, 0), (OUT, 7, 1), (AWAY, 1, 0), (CORES, 0, 7), (HERE, 1, 1),
+    (BACK, 7, 0), (FIRST, 0, 7), (BACK, 7, 1), (CORES, 1, 7), (HERE, 0, 0), (FIRST, 1, 7),
+    (THIRD, 1, 1), (HERE, 1, 0), (THIRD, 1, 0), (THIRD, 0, 0),
+)
+
+
 def mixture_kernel(
     sizes,
-    block_ref,
+    part_ref,
     cot_ref,
     expert_in_ref,
     shared_in_ref,
@@ -652,11 +688,18 @@
     shared_out_ref,
     select_ref,
     place_ref,
-    residual_ref,
+    tokens_ref,
+    gain_ref,
+    router_ref,
+    picked_ref,
     output_ref,
-    sum_ref,
+    block_ref,
+    residual_grad_ref,
+    logit_grad_ref,
+    gain_grad_ref,
     rows_ref,
     units_ref,
+    residual_all_ref,
     weight_in,
     weight_out,
     rows_buf,
@@ -665,9 +708,10 @@
     dots,
     staged_out,
     staged_back,
+    gates,
     *rest,
 ):
-    rows, seq, width, owned, part, shared_part, padded = sizes
+    rows, seq, width, owned, part, shared_part, padded, experts = sizes
     out_slots, back_slots = rest[:6], rest[6:12]
     send_sems, recv_sems, load_sems, misc_sems = rest[12:]
     bf16, f32 = jnp.bfloat16, jnp.float32
@@ -679,7 +723,24 @@
     both = (sums_out, sums_back)
 
     own = pltpu.make_async_copy(block_ref, gather.view(0, 0, 0, None), misc_sems.at[0])
-    own.start()
+    attended = sums_out.staged_part(part_ref)
+    mine = [
+        pltpu.make_async_copy(
+            attended(ky, 0),
+            staged_back.at[pl.ds(ky * rows, rows), pl.ds(0, width)],
+            misc_sems.at[4 + ky],
+        )
+        for ky in (0, 1)
+    ]
+    mine.append(
+        pltpu.make_async_copy(
+            tokens_ref,
+            staged_back.at[pl.ds(2 * rows, rows), pl.ds(0, width)],
+            misc_sems.at[6],
+        )
+    )
+    for load in mine:
+        load.start()
     moves = []
     for c in (0, 1):
         for e in range(owned):
@@ -704,7 +765,7 @@
     for load in loads:
         load.start()
 
-    order = [(0, 1), (1, 1), (1, 0), (2, 1), (2, 0), (3, 1), (3, 0), (0, 0)]
+    order = ORDER
 
     def span(step):
         return pl.ds(pl.multiple_of(place.sequence(*order[step]) * seq, seq), seq)
@@ -719,23 +780,51 @@
         return pltpu.make_async_copy(units_buf, units_ref.at[span(step)], misc_sems.at[3])
 
     cot_load(0).start()
-    greet(place, PARTNERS)
-    gather.first(0)
-    gather.begin(1)
     used = owned * part + shared_part
     for at in (used, padded + used):
         weight_in[pl.ds(at, padded - used), :] = jnp.zeros((padded - used, width), bf16)
     weight_out[pl.ds(used, padded - used), :] = jnp.zeros((padded - used, width), bf16)
-    gather.second_x(0)
-    gather.second_y(0)
-    gather.begin(2)
-    gather.third(0)
-    gather.first(1)
-    own.wait()
-    gather.have(0, 1)
-    rows_load(0).start()
-    for load in loads:
-        load.wait()
+    greet(place, PARTNERS)
+
+    def third_of(ref, i):
+        return ref.at[pl.ds(i * rows, rows), pl.ds(0, width)]
+
+    for ky in (1, 0):
+        copies.start(("pc", ky), attended(ky, 1), third_of(staged_out, ky), kc=1)
+    mine[1].wait()
+    copies.arrived(("pc", 1))
+    third_of(staged_out, 1)[...] = third_of(staged_out, 1)[...] + third_of(staged_back, 1)[...]
+    copies.start(("py", 0), third_of(staged_out, 1), third_of(staged_out, 2), ky=1)
+    mine[0].wait()
+    copies.arrived(("pc", 0))
+    total = third_of(staged_out, 0)[...].astype(f32) + third_of(staged_back, 0)[...].astype(f32)
+    mine[2].wait()
+    total = total + third_of(staged_back, 2)[...].astype(f32)
+    copies.arrived(("py", 0))
+    total = total + third_of(staged_out, 2)[...].astype(f32)
+    residual_grad_ref[...] = total
+    factor = lax.rsqrt(jnp.mean(total * total, axis=-1, keepdims=True) + EPSILON)
+    block_ref[:, pl.ds(0, width)] = (total * factor * gain_ref[...]).astype(bf16)
+    logits = lax.dot_general(
+        block_ref[:, pl.ds(0, width)], router_ref[...], NT_DIMS, preferred_element_type=f32
+    )
+    lane = lax.broadcasted_iota(jnp.int32, (rows, EXTRA), 1)
+    routed = lane < experts
+    highest = jnp.max(jnp.where(routed, logits, MASKED), axis=-1, keepdims=True)
+    raised = jnp.where(routed, jnp.exp(jnp.where(routed, logits, highest) - highest), 0.0)
+    probs = raised / jnp.sum(raised, axis=-1, keepdims=True)
+    gates[...] = jnp.where(lane == experts, jax.nn.sigmoid(logits), probs)
+    weights = jnp.where(routed, probs * picked_ref[...], gates[...])
+    coarse = weights.astype(bf16)
+    fine = (weights - coarse.astype(f32)).astype(bf16)
+    across = lax.broadcasted_iota(jnp.int32, (EXTRA, EXTRA), 1)
+    down = lax.broadcasted_iota(jnp.int32, (EXTRA, EXTRA), 0)
+    moved = jnp.where(across == down + experts + 1, 1.0, 0.0).astype(bf16)
+    block_ref[:, pl.ds(width, EXTRA)] = (
+        coarse.astype(f32) + jnp.dot(fine, moved, preferred_element_type=f32)
+    ).astype(bf16)
+    copies.sent(("py", 0))
+    own.start()
 
     def raise_tile(at, count):
         here, above = pl.ds(at, count), pl.ds(at + padded, count)
@@ -765,129 +854,139 @@
 
     tile, wide = 256, 512
 
-    def raise_and_back():
-        dots[...] = jnp.zeros_like(dots)
-
-        @pl.loop(0, padded // tile)
-        def _(j):
-            raise_tile(pl.multiple_of(j * tile, tile), tile)
-
-        if padded % tile:
-            raise_tile(padded // tile * tile, padded % tile)
-
-    def project_out():
-        @pl.loop(0, width // wide)
+    tiles = padded // tile
+    pieces = tiles + (1 if padded % tile else 0)
+    strips = width // wide // 2
+
+    def raise_some(step, first, last):
+        if first == 0:
+            rows_load(step).wait()
+            cot_load(step).wait()
+            if step:
+                units_write(step - 1).wait()
+            else:
+                for load in loads:
+                    load.wait()
+            dots[...] = jnp.zeros_like(dots)
+        if min(last, tiles) - first == 1:
+            raise_tile(first * tile, tile)
+        elif min(last, tiles) > first:
+
+            @pl.loop(first, min(last, tiles))
+            def _(j):
+                raise_tile(pl.multiple_of(j * tile, tile), tile)
+
+        if last > tiles:
+            raise_tile(tiles * tile, padded % tile)
+        if last == pieces:
+            units_write(step).start()
+            if step + 1 < len(order):
+                cot_load(step + 1).start()
+
+    def project(first, last, units, weight, staged):
+        @pl.loop(first * strips, last * strips)
         def _(n):
             at = pl.ds(pl.multiple_of(n * wide, wide), wide)
-            staged_out[:, at] = jnp.dot(
-                units_buf[:, pl.ds(2 * padded, padded)],
-                weight_out[:, at],
-                preferred_element_type=f32,
+            staged[:, at] = jnp.dot(
+                units_buf[:, units], weight[:, at], preferred_element_type=f32
             ).astype(bf16)
 
-    def project_back():
-        @pl.loop(0, width // wide)
-        def _(n):
-            at = pl.ds(pl.multiple_of(n * wide, wide), wide)
-            staged_back[:, at] = jnp.dot(
-                units_buf[:, pl.ds(0, 2 * padded)], weight_in[:, at], preferred_element_type=f32
-            ).astype(bf16)
-
-        staged_back[:, pl.ds(width, EXTRA)] = dots[...].astype(bf16)
-
-    def sums_first(done):
-        sums_out.first(*order[done], sums_out.staged_part(staged_out))
-        sums_back.first(*order[done], sums_back.staged_part(staged_back))
-
-    def second_gather(kz):
-        gather.second_y(kz)
-        gather.second_x(kz)
-
-    def next_rows(step):
-        if step + 1 < len(order):
-            gather.have(*order[step + 1])
-            rows_load(step + 1).start()
-
-    def after_raise(step):
-        if step:
-            sums_first(step - 1)
-        if step == 0:
-            second_gather(1)
-            gather.begin(3)
-        elif step == 1:
-            gather.first(2)
-        elif step == 2:
-            gather.third(2)
-            gather.first(3)
-            for sums in both:
-                sums.second_away(0)
-        elif step == 3:
-            second_gather(3)
-            for sums in both:
-                sums.second_away(1)
-        elif step == 4:
-            gather.third(3)
-            for sums in both:
-                sums.second_here(1)
-        elif step == 5:
-            for sums in both:
-                sums.second_away(2)
-            for sums in both:
-                sums.third(1)
-        elif step == 6:
-            for sums in both:
-                sums.second_here(2)
-        elif step == 7:
-            for sums in both:
-                sums.second_away(3)
-            for sums in both:
-                sums.third(2)
-
-    def after_out(step):
-        if step == 0:
-            gather.third(1)
+    def out_some(step, first, last):
+        project(first, last, pl.ds(2 * padded, padded), weight_out, staged_out)
+
+    def back_some(step, first, last):
+        project(first, last, pl.ds(0, 2 * padded), weight_in, staged_back)
+        if last == 2:
+            staged_back[:, pl.ds(width, EXTRA)] = dots[...].astype(bf16)
+
+    def have(step):
+        if order[step] == (0, 0):
+            own.wait()
+        gather.have(*order[step])
+        rows_load(step).start()
+
+    work = {RAISE: raise_some, OUT: out_some, BACK: back_some}
+    moves = {
+        BEGIN: gather.begin,
+        PASS: gather.first,
+        PASS_X: gather.second_x,
+        PASS_Y: gather.second_y,
+        PASS_LAST: gather.third,
+        HAVE: have,
+    }
+    stages = (staged_out, staged_back)
+    at = 0
+    while at < len(PLAN):
+        kind, a, b = PLAN[at]
+        at += 1
+        if kind in work:
+            last = b + 1
+            while at < len(PLAN) and PLAN[at] == (kind, a, last):
+                last, at = last + 1, at + 1
+            work[kind](a, b, last)
+        elif kind in moves:
+            moves[kind](a)
+        elif kind == CORES:
+            both[a].cores(*order[b], both[a].staged_part(stages[a]))
+        elif kind == FIRST:
+            both[a].first(*order[b], both[a].staged_part(stages[a]))
+        elif kind == AWAY:
+            both[a].second_away(b)
+        elif kind == HERE:
+            both[a].second_here(b)
         else:
-            next_rows(step)
-
-    def after_back(step):
-        if step == 0:
-            next_rows(step)
-        elif step == 1:
-            second_gather(2)
-        elif step == 7:
-            for sums in both:
-                sums.second_here(3)
-
-    for step in range(len(order)):
-        rows_load(step).wait()
-        cot_load(step).wait()
-        if step:
-            units_write(step - 1).wait()
-        raise_and_back()
-        units_write(step).start()
-        if step + 1 < len(order):
-            cot_load(step + 1).start()
-        after_raise(step)
-        project_out()
-        sums_out.cores(*order[step], sums_out.staged_part(staged_out))
-        after_out(step)
-        project_back()
-        sums_back.cores(*order[step], sums_back.staged_part(staged_back))
-        after_back(step)
+            both[a].third(b)
     last = len(order) - 1
-    sums_first(last)
-    for sums in both:
-        sums.third(3)
-    for sums in both:
-        sums.second_here(0)
-    for sums in both:
-        sums.third(0)
-    output_ref[...] = (residual_ref[...] + sums_out.total()).astype(bf16)
-    sum_ref[...] = sums_back.total()
+    own_cot = pltpu.make_async_copy(
+        cot_ref.at[pl.ds(pl.multiple_of(place.block(0, 0, 0, 0) * rows, rows), rows)],
+        cot_buf.at[pl.ds(0, rows)],
+        misc_sems.at[7],
+    )
+    own_cot.start()
+    total = residual_grad_ref[...]
+    output_ref[...] = (total + sums_out.total()).astype(bf16)
+    own_cot.wait()
+    back = sums_back.total()
+    factor = lax.rsqrt(jnp.mean(total * total, axis=-1, keepdims=True) + EPSILON)
+    normed = total * factor
+    held = gates[...]
+    extra = back[:, width:]
+    pick_grads = jnp.where(routed, extra * picked_ref[...], 0.0)
+    probs = jnp.where(routed, held, 0.0)
+    inner = jnp.sum(pick_grads * probs, axis=-1, keepdims=True)
+    logit_grad = jnp.where(
+        lane == experts, extra * held * (1.0 - held), probs * (pick_grads - inner)
+    ).astype(bf16)
+    logit_grad_ref[...] = logit_grad
+    second_grad = back[:, :width] + jnp.dot(
+        logit_grad, router_ref[...], preferred_element_type=f32
+    )
+    scaled = second_grad * gain_ref[...]
+    inner = jnp.mean(scaled * normed, axis=-1, keepdims=True)
+    cotangent = cot_buf[pl.ds(0, rows), :].astype(f32)
+    residual_grad = cotangent + factor * (scaled - normed * inner)
+    residual_grad_ref[...] = residual_grad
+    gain_grad_ref[...] = jnp.sum(second_grad * normed, axis=0, keepdims=True)
+    for ky in (0, 1):
+        copies.sent((SUM_CORES, 0) + order[last] + (ky,))
+    third_of(staged_out, 0)[...] = residual_grad.astype(bf16)
+
+    def spot(ky, kc):
+        start = (place.y_of(ky) * 2 + place.c_of(kc)) * rows
+        return residual_all_ref.at[pl.ds(pl.multiple_of(start, rows), rows)]
+
+    shown = pltpu.make_async_copy(third_of(staged_out, 0), spot(0, 0), misc_sems.at[6])
+    shown.start()
+    copies.start(("gy", 0), third_of(staged_out, 0), spot(0, 0), ky=1)
+    copies.start(("gc", 0), third_of(staged_out, 0), spot(0, 0), kc=1)
+    copies.arrived(("gy", 0))
+    copies.start(("gf", 0), spot(1, 0), spot(1, 0), kc=1)
     units_write(last).wait()
+    copies.arrived(("gc", 0))
+    copies.arrived(("gf", 0))
+    shown.wait()
     for name in copies.made:
-        if name[0] != SUM_CORES:
-            copies.sent(name)
+        copies.sent(name)
 
 
 def sum_slots(rows, packed):
@@ -904,31 +1003,47 @@
 
 
 def mixture(
-    row_pack, cot_all, expert_in, shared_win, expert_out, shared_wout, select, spots, residual
+    attn_part,
+    cot_all,
+    expert_in,
+    shared_win,
+    expert_out,
+    shared_wout,
+    select,
+    spots,
+    tokens,
+    gain,
+    router_wide,
+    picked,
+    experts,
 ):
-    rows, packed = row_pack.shape
-    width = packed - EXTRA
+    rows, width = tokens.shape
+    packed = width + EXTRA
     total_rows = cot_all.shape[0]
     owned, part = expert_out.shape[0], expert_out.shape[1]
     shared_part = shared_wout.shape[0]
-    seq = total_rows // lax.axis_size(EXPERT)
+    seq = attn_part.shape[0]
     padded = select.shape[1]
     bf16, f32 = jnp.bfloat16, jnp.float32
     vmem = pl.BlockSpec(memory_space=pltpu.VMEM)
     anywhere = pl.BlockSpec(memory_space=pl.ANY)
-    copies = GATHER_COPIES + 2 * SUM_COPIES
+    copies = GATHER_COPIES + 2 * SUM_COPIES + 6
     return pl.pallas_call(
         functools.partial(
-            mixture_kernel, (rows, seq, width, owned, part, shared_part, padded)
+            mixture_kernel, (rows, seq, width, owned, part, shared_part, padded, experts)
         ),
         out_shape=(
             jax.ShapeDtypeStruct((rows, width), bf16),
-            jax.ShapeDtypeStruct((rows, packed), f32),
+            jax.ShapeDtypeStruct((rows, packed), bf16),
+            jax.ShapeDtypeStruct((rows, width), f32),
+            jax.ShapeDtypeStruct((rows, EXTRA), bf16),
+            jax.ShapeDtypeStruct((1, width), f32),
             jax.ShapeDtypeStruct((total_rows, packed), bf16),
             jax.ShapeDtypeStruct((total_rows, 3 * padded), bf16),
+            jax.ShapeDtypeStruct((seq, width), bf16),
         ),
-        in_specs=[anywhere] * 6 + [vmem] * 3,
-        out_specs=(vmem,) * 2 + (anywhere,) * 2,
+        in_specs=[anywhere] * 6 + [vmem] * 2 + [anywhere] + [vmem] * 3,
+        out_specs=(vmem,) * 5 + (anywhere,) * 3,
         scratch_shapes=[
             pltpu.VMEM((2 * padded, width), bf16),
             pltpu.VMEM((padded, width), bf16),
@@ -938,6 +1053,7 @@
             pltpu.VMEM((seq, EXTRA), f32),
             pltpu.VMEM((seq, width), bf16),
             pltpu.VMEM((seq, packed), bf16),
+            pltpu.VMEM((rows, EXTRA), f32),
         ]
         + sum_slots(rows, width)
         + sum_slots(rows, packed)
@@ -945,7 +1061,7 @@
             pltpu.SemaphoreType.DMA((copies,)),
             pltpu.SemaphoreType.DMA((copies,)),
             pltpu.SemaphoreType.DMA((2 * owned + 4,)),
-            pltpu.SemaphoreType.DMA((4,)),
+            pltpu.SemaphoreType.DMA((8,)),
         ],
         compiler_params=pltpu.CompilerParams(
             collective_id=0, has_side_effects=True, vmem_limit_bytes=63 * 2**20
@@ -957,7 +1073,7 @@
         ),
         name="mixture",
     )(
-        row_pack,
+        attn_part,
         cot_all,
         expert_in.transpose(0, 2, 3, 1).reshape(2 * owned * part, width),
         shared_win,
@@ -965,7 +1081,10 @@
         shared_wout,
         select,
         spots,
-        residual,
+        tokens,
+        gain,
+        router_wide,
+        picked,
     )
 
 
@@ -1013,7 +1132,7 @@
     def load(self, kz):
         return [
             pltpu.make_async_copy(
-                self.view(i, kz, 0), self.mine[i].at[kz % 2], self.sems.at[2 * (kz % 2) + i]
+                self.view(i, kz, 0), self.mine[i].at[kz], self.sems.at[2 * kz + i]
             )
             for i in (0, 1)
         ]
@@ -1024,19 +1143,45 @@
         for i in (0, 1):
             self.copies.arrived(("ox", i, kz))
             held = self.from_x[i].at[kz]
-            held[...] = held[...] + self.mine[i][kz % 2]
-            if kz:
-                self.copies.start(("oz", i, kz), held, self.from_z[i].at[kz - 1], kz=kz)
+            held[...] = held[...] + self.mine[i][kz]
+            if kz in (1, 3):
+                self.copies.start(("oz", i, kz), held, self.from_z[i].at[kz // 2], kz=1)
+
+    def relay(self):
+        for i in (0, 1):
+            self.copies.arrived(("oz", i, 3))
+            held = self.from_x[i].at[2]
+            held[...] = held[...] + self.from_z[i][1]
+            self.copies.start(("oz", i, 2), held, self.from_z[i].at[2], kz=2)
 
     def finish(self, i, out_ref):
         total = self.from_x[i][0].astype(jnp.float32)
-        for kz in (1, 2, 3):
+        for kz, slot in ((1, 0), (2, 2)):
             self.copies.arrived(("oz", i, kz))
-            total = total + self.from_z[i][kz - 1].astype(jnp.float32)
+            total = total + self.from_z[i][slot].astype(jnp.float32)
         out_ref[...] = total
 
 
-CLOSING_COPIES = 14 + 14 + 6
+CLOSING_COPIES = 14 + 14 + 6 + 3
+TURN, PRODUCT, GIVE, BEGIN_X, ADD, RELAY, TOTALS, PASS_FIRST, END_FIRST = range(9)
+CLOSING_ORDER = (2, 3, 1, 0)
+CLOSING_PLAN = (
+    (TURN, 0, 0, 0), (PASS_FIRST, 0, 0, 0), (TURN, 1, 0, 0), (BEGIN_X, 3, 0, 0), (TURN, 2, 0, 0),
+    (TURN, 3, 0, 0), (TURN, 4, 0, 0), (TURN, 5, 0, 0), (TURN, 6, 0, 0), (TURN, 7, 0, 0),
+    (TURN, 8, 0, 0), (END_FIRST, 0, 0, 0), (TOTALS, 0, 0, 0), (TURN, 9, 0, 0), (TURN, 10, 0, 0),
+    (TURN, 11, 0, 0), (TURN, 12, 0, 0), (TOTALS, 1, 0, 0), (TURN, 13, 0, 0), (TURN, 14, 0, 0),
+    (TURN, 15, 0, 0), (TURN, 16, 0, 0), (BEGIN_X, 2, 0, 0), (TURN, 17, 0, 0), (TURN, 18, 0, 0),
+    (TOTALS, 2, 0, 0), (TURN, 19, 0, 0), (TURN, 20, 0, 0), (BEGIN_X, 1, 0, 0), (ADD, 3, 0, 0),
+    (PRODUCT, 2, 0, 0), (PRODUCT, 2, 0, 1), (PRODUCT, 2, 1, 0), (PRODUCT, 2, 1, 1),
+    (GIVE, 0, 2, 0), (TOTALS, 3, 0, 0), (PRODUCT, 2, 2, 0), (PRODUCT, 2, 2, 1), (GIVE, 1, 2, 0),
+    (PRODUCT, 3, 0, 0), (PRODUCT, 3, 0, 1), (PRODUCT, 3, 1, 0), (PRODUCT, 3, 1, 1),
+    (GIVE, 0, 3, 0), (PRODUCT, 3, 2, 0), (PRODUCT, 3, 2, 1), (GIVE, 1, 3, 0), (PRODUCT, 1, 0, 0),
+    (PRODUCT, 1, 0, 1), (PRODUCT, 1, 1, 0), (PRODUCT, 1, 1, 1), (GIVE, 0, 1, 0), (ADD, 2, 0, 0),
+    (PRODUCT, 1, 2, 0), (RELAY, 0, 0, 0), (PRODUCT, 1, 2, 1), (ADD, 1, 0, 0), (BEGIN_X, 0, 0, 0),
+    (GIVE, 1, 1, 0), (PRODUCT, 0, 0, 0), (PRODUCT, 0, 0, 1), (PRODUCT, 0, 1, 0),
+    (PRODUCT, 0, 1, 1), (GIVE, 0, 0, 0), (ADD, 0, 0, 0), (PRODUCT, 0, 2, 0), (PRODUCT, 0, 2, 1),
+    (GIVE, 1, 0, 0),
+)
 
 
 def closing_kernel(
@@ -1046,7 +1191,12 @@
     units_ref,
     att_in_ref,
     att_out_ref,
+    first_ref,
     small_ref,
+    tokens_ref,
+    residual_grad_ref,
+    gain_ref,
+    input_grad_ref,
     att_in_out,
     att_out_out,
     small_out,
@@ -1071,6 +1221,8 @@
     small_y,
     small_x,
     small_z,
+    first_mine,
+    first_got,
     send_sems,
     recv_sems,
     own_sems,
@@ -1079,7 +1231,8 @@
     write_sems,
     keep_sems,
 ):
-    width, owned, part, shared_part, owner_width, padded = sizes
+    width, owned, part, shared_part, owner_width, padded, gain_row = sizes
+    rows = tokens_ref.shape[0]
     f32, bf16 = jnp.float32, jnp.bfloat16
     place = Place()
     copies = Copies(place, send_sems, recv_sems)
@@ -1109,19 +1262,31 @@
         at = pl.ds(pl.multiple_of(place.z_of(kz) * wide, wide), wide)
         return pltpu.make_async_copy(source.at[:, at], columns.at[which], column_sems.at[which])
 
+    order = CLOSING_ORDER
     chunk_load(0, 0).start()
-    for load in owners.load(3) + owners.load(2):
+    for kz in range(4):
+        for load in owners.load(kz):
+            load.start()
+    small[...] = small_ref[...]
+
+    def first_part(ky, kc):
+        start = (place.y_of(ky) * 2 + place.c_of(kc)) * rows
+        return first_ref.at[pl.ds(pl.multiple_of(start, rows), rows)]
+
+    first_loads = [
+        pltpu.make_async_copy(first_part(ky, 0), first_mine.at[ky], keep_sems.at[2 + ky])
+        for ky in (0, 1)
+    ]
+    for load in first_loads:
         load.start()
-    small[...] = small_ref[...]
     greet(place, PARTNERS + FARTHER)
-    totals.send(CORE)
-    owners.begin(3)
-    owners.begin(2)
-    column_load(3, 0).start()
-    column_load(3, 1).start()
-
-    def turn(kind):
-        @pl.loop(kind * per_kind, (kind + 1) * per_kind)
+    for ky in (1, 0):
+        copies.start(("fc", ky), first_part(ky, 1), first_got.at[ky], kc=1)
+    column_load(order[0], 0).start()
+    column_load(order[0], 1).start()
+
+    def turn(first, last):
+        @pl.loop(first, last)
         def _(i):
             slot = i % 2
             chunk_load(i, slot).wait()
@@ -1136,13 +1301,6 @@
             def _(r):
                 at = pl.ds(pl.multiple_of(r * wide, wide), wide)
                 turned[to, at] = chunks[slot, at, :].T
-
-    def owners_add(kz):
-        owners.add(kz)
-        if kz >= 2:
-            for load in owners.load(kz - 2):
-                load.start()
-            owners.begin(kz - 2)
 
     def span(kz):
         return pl.ds(pl.multiple_of(place.z_of(kz) * wide, wide), wide)
@@ -1172,15 +1330,16 @@
             else:
                 pltpu.make_async_copy(source, target, keep_sems.at[which]).start()
 
-    def product(kz, kind):
-        which = kind // 2
-        if kind != 1:
-            column_load(kz, which).wait()
-        if kz < 3:
-            for write in writes(kz + 1, kind):
-                write.wait()
-
-        @pl.loop(0, 2)
+    def product(kz, kind, first, last):
+        which, step = kind // 2, order.index(kz)
+        if first == 0:
+            if kind != 1:
+                column_load(kz, which).wait()
+            if step:
+                for write in writes(order[step - 1], kind):
+                    write.wait()
+
+        @pl.loop(first, last)
         def _(n):
             at = pl.ds(pl.multiple_of(n * owner_width, owner_width), owner_width)
             grads[kind, :, at] = jnp.dot(
@@ -1189,8 +1348,10 @@
                 preferred_element_type=f32,
             ).astype(bf16)
 
-        if kz and kind:
-            column_load(kz - 1, which).start()
+        if last < 2:
+            return
+        if step < 3 and kind:
+            column_load(order[step + 1], which).start()
         for write in writes(kz, kind):
             write.start()
         shared = grads[kind, pl.ds(cut, shared_part), :]
@@ -1198,39 +1359,70 @@
             shared_in_send[kz, pl.ds(kind * shared_part, shared_part), :] = shared
         else:
             shared_out_send[kz] = shared
-        if kind:
-            share(kz, which)
-
-    turn(0)
-    totals.add(CORE)
-    totals.send(ROW)
-    turn(1)
-    owners_add(3)
-    turn(2)
-    totals.add(ROW)
-    totals.send(COLUMN)
-    product(3, 0)
-    product(3, 1)
-    owners_add(2)
-    product(3, 2)
-    totals.add(COLUMN)
-    totals.send_z()
-    product(2, 0)
-    product(2, 1)
-    product(2, 2)
-    owners_add(1)
-    product(1, 0)
-    product(1, 1)
-    product(1, 2)
-    owners_add(0)
-    product(0, 0)
-    product(0, 1)
-    product(0, 2)
+
+    def pass_first():
+        first_loads[1].wait()
+        copies.arrived(("fc", 1))
+        first_got[1] = first_got[1] + first_mine[1]
+        copies.start(("fy", 0), first_got.at[1], first_got.at[2], ky=1)
+
+    def end_first():
+        first_loads[0].wait()
+        copies.arrived(("fc", 0))
+        copies.arrived(("fy", 0))
+        grad = first_got[0].astype(f32) + first_mine[0].astype(f32)
+        grad = grad + first_got[2].astype(f32)
+        inputs = tokens_ref[...].astype(f32)
+        factor = lax.rsqrt(jnp.mean(inputs * inputs, axis=-1, keepdims=True) + EPSILON)
+        normed = inputs * factor
+        scaled = grad * gain_ref[...]
+        inner = jnp.mean(scaled * normed, axis=-1, keepdims=True)
+        input_grad_ref[...] = residual_grad_ref[...] + factor * (scaled - normed * inner)
+        small[pl.ds(gain_row, 1), :] = jnp.sum(grad * normed, axis=0, keepdims=True)
+
+    axes = (CORE, ROW, COLUMN)
+
+    def totals_step(n):
+        if n:
+            totals.add(axes[n - 1])
+        if n < 3:
+            totals.send(axes[n])
+        else:
+            totals.send_z()
+
+    at = 0
+    while at < len(CLOSING_PLAN):
+        kind, a, b, c = CLOSING_PLAN[at]
+        at += 1
+        if kind == TURN:
+            last = a + 1
+            while CLOSING_PLAN[at] == (TURN, last, 0, 0):
+                last, at = last + 1, at + 1
+            turn(a, last)
+        elif kind == PRODUCT:
+            last = c + 1
+            if CLOSING_PLAN[at] == (PRODUCT, a, b, last):
+                last, at = last + 1, at + 1
+            product(a, b, c, last)
+        elif kind == GIVE:
+            share(b, a)
+        elif kind == BEGIN_X:
+            owners.begin(a)
+        elif kind == ADD:
+            owners.add(a)
+        elif kind == RELAY:
+            owners.relay()
+        elif kind == PASS_FIRST:
+            pass_first()
+        elif kind == END_FIRST:
+            end_first()
+        else:
+            totals_step(a)
     small_out[...] = totals.finish()
     owners.finish(0, att_in_out)
     owners.finish(1, att_out_out)
     for kind in (0, 1, 2):
-        for write in writes(0, kind):
+        for write in writes(order[-1], kind):
             write.wait()
     for which in (0, 1):
         sent = (shared_in_send, shared_out_send)[which]
@@ -1241,12 +1433,27 @@
         if name[0] == SHARE:
             copies.arrived(name)
     for name in copies.made:
-        if name[0] != TOTAL:
-            copies.sent(name)
-
-
-def closing(rows_all, cot_all, units_all, att_in, att_out, small, owned, part, shared_part):
+        copies.sent(name)
+
+
+def closing(
+    rows_all,
+    cot_all,
+    units_all,
+    att_in,
+    att_out,
+    first_rows,
+    small,
+    tokens,
+    residual_grad,
+    gain,
+    gain_row,
+    owned,
+    part,
+    shared_part,
+):
     total_rows, width = cot_all.shape
+    rows = tokens.shape[0]
     padded = units_all.shape[1] // 3
     owners = lax.axis_size(EXPERT)
     owner_width = width // owners
@@ -1259,9 +1466,10 @@
     block_out = (heads_width, owner_width)
     return pl.pallas_call(
         functools.partial(
-            closing_kernel, (width, owned, part, shared_part, owner_width, padded)
+            closing_kernel, (width, owned, part, shared_part, owner_width, padded, gain_row)
         ),
         out_shape=(
+            jax.ShapeDtypeStruct((rows, width), f32),
             jax.ShapeDtypeStruct(block_in, f32),
             jax.ShapeDtypeStruct(block_out, f32),
             jax.ShapeDtypeStruct(small.shape, f32),
@@ -1270,8 +1478,8 @@
             jax.ShapeDtypeStruct((owners, 2 * shared_part, owner_width), bf16),
             jax.ShapeDtypeStruct((owners, shared_part, owner_width), bf16),
         ),
-        in_specs=[anywhere] * 5 + [vmem],
-        out_specs=(vmem,) * 3 + (anywhere,) * 4,
+        in_specs=[anywhere] * 6 + [vmem] * 4,
+        out_specs=(vmem,) * 4 + (anywhere,) * 4,
         scratch_shapes=[
             pltpu.VMEM((2, total_rows, 128), bf16),
             pltpu.VMEM((3 * padded, total_rows), bf16),
@@ -1279,8 +1487,8 @@
             pltpu.VMEM((3, padded, wide), bf16),
             pltpu.VMEM((4, 2 * shared_part, wide), bf16),
             pltpu.VMEM((4, shared_part, wide), bf16),
-            pltpu.VMEM((2,) + block_in, bf16),
-            pltpu.VMEM((2,) + block_out, bf16),
+            pltpu.VMEM((4,) + block_in, bf16),
+            pltpu.VMEM((4,) + block_out, bf16),
             pltpu.VMEM((4,) + block_in, bf16),
             pltpu.VMEM((4,) + block_out, bf16),
             pltpu.VMEM((3,) + block_in, bf16),
@@ -1289,13 +1497,15 @@
         + [pltpu.VMEM(small.shape, f32)] * 4
         + [
             pltpu.VMEM((4,) + small.shape, f32),
+            pltpu.VMEM((2, rows, width), bf16),
+            pltpu.VMEM((3, rows, width), bf16),
             pltpu.SemaphoreType.DMA((CLOSING_COPIES,)),
             pltpu.SemaphoreType.DMA((CLOSING_COPIES,)),
-            pltpu.SemaphoreType.DMA((4,)),
+            pltpu.SemaphoreType.DMA((8,)),
             pltpu.SemaphoreType.DMA((2,)),
             pltpu.SemaphoreType.DMA((2,)),
             pltpu.SemaphoreType.DMA((3 * owned,)),
-            pltpu.SemaphoreType.DMA((2,)),
+            pltpu.SemaphoreType.DMA((4,)),
         ],
         compiler_params=pltpu.CompilerParams(
             collective_id=1, has_side_effects=True, vmem_limit_bytes=62 * 2**20
@@ -1306,10 +1516,33 @@
             transcendentals=0,
         ),
         name="closing",
-    )(rows_all, cot_all, units_all, att_in, att_out, small)
-
-
-OPENING_COPIES = 6 + 8 + 3 + 14
+    )(
+        rows_all,
+        cot_all,
+        units_all,
+        att_in,
+        att_out,
+        first_rows,
+        small,
+        tokens,
+        residual_grad,
+        gain,
+    )
+
+
+OPENING_COPIES = 6 + 8 + 3 + 14 + 31
+SPREAD_Z, RELAY_Z, PASS_ON_X, SLICES, NORMED = range(5)
+COT_Z, COT_RELAY, COT_X, COT_Y, COT_CORE = range(5, 10)
+OPENING_PLAN = (
+    (SPREAD_Z, 1, 0), (COT_X, 0, 0), (COT_Z, 2, 0), (PASS_ON_X, 0, 0), (COT_X, 2, 0),
+    (PASS_ON_X, 1, 0), (COT_Z, 1, 0), (SPREAD_Z, 2, 0), (COT_Y, 2, 0), (COT_Y, 0, 1),
+    (SLICES, 2, 1), (COT_Y, 2, 1), (COT_X, 1, 0), (COT_RELAY, 0, 0), (COT_Y, 1, 0),
+    (COT_CORE, 2, 0), (COT_Y, 0, 0), (COT_X, 3, 0), (SLICES, 1, 0), (COT_CORE, 1, 0),
+    (COT_Y, 1, 1), (SLICES, 0, 1), (RELAY_Z, 0, 0), (COT_CORE, 0, 0), (PASS_ON_X, 2, 0),
+    (COT_Y, 3, 0), (SLICES, 3, 1), (COT_Y, 3, 1), (COT_CORE, 3, 1), (COT_CORE, 0, 1),
+    (COT_CORE, 2, 1), (SLICES, 2, 0), (NORMED, 0, 0), (COT_CORE, 1, 1), (SLICES, 1, 1),
+    (SLICES, 3, 0), (PASS_ON_X, 3, 0), (COT_CORE, 3, 0),
+)
 
 
 def opening_kernel(
@@ -1319,11 +1552,13 @@
     att_out_ref,
     shared_in_ref,
     shared_out_ref,
+    cot_ref,
     normed_all,
     att_in_all,
     att_out_all,
     shared_in_all,
     shared_out_all,
+    cot_all,
     send_sems,
     recv_sems,
     own_sems,
@@ -1352,10 +1587,15 @@
             (shared_out_ref.at[at], shared_out_all.at[:, here]),
         )
 
+    def cot_view(kz, kx, ky):
+        start = place.block(kz, kx, ky, 0) * rows
+        return cot_all.at[pl.ds(pl.multiple_of(start, rows), rows)]
+
     keeps = [
         (normed_ref, normed_all.at[spot]),
         (att_in_ref, in_view(0, 0)),
         (att_out_ref, out_view(0, 0)),
+        (cot_ref, cot_view(0, 0, 0)),
     ] + list(shared_block(0, 0))
     keeps = [
         pltpu.make_async_copy(source, target, own_sems.at[i])
@@ -1365,11 +1605,17 @@
         keep.start()
     greet(place, PARTNERS + FARTHER + [dict(ky=1, kc=1)])
 
-    def spread_z(kz):
+    def spread_z(kz, _):
         copies.start(("zi", kz), att_in_ref, in_view(0, 0), kz=kz)
         copies.start(("zo", kz), att_out_ref, out_view(0, 0), kz=kz)
 
-    def pass_x(kz):
+    def relay_z(_, __):
+        copies.arrived(("zi", 2))
+        copies.start(("zi", 3), in_view(2, 0), in_view(2, 0), kz=1)
+        copies.arrived(("zo", 2))
+        copies.start(("zo", 3), out_view(2, 0), out_view(2, 0), kz=1)
+
+    def pass_x(kz, _):
         if kz:
             copies.arrived(("zi", kz))
         source = in_view(kz, 0) if kz else att_in_ref
@@ -1379,36 +1625,66 @@
         source = out_view(kz, 0) if kz else att_out_ref
         copies.start(("xo", kz), source, out_view(kz, 0), kx=1)
 
-    def share(kz, kx):
+    def slices(kz, kx):
         for which, (source, target) in enumerate(shared_block(kz, kx)):
             copies.start((SHARE, which, kz, kx), source, target, kz=kz, kx=kx)
 
-    spread_z(1)
-    pass_x(0)
-    spread_z(2)
-    for ky, kc in ((0, 1), (1, 0), (1, 1)):
-        copies.start(("n", ky, kc), normed_ref, normed_all.at[spot], ky=ky, kc=kc)
-    pass_x(1)
-    spread_z(3)
-    pass_x(2)
-    share(1, 0)
-    share(1, 1)
-    pass_x(3)
-    share(3, 0)
-    share(3, 1)
-    share(2, 0)
-    share(2, 1)
-    share(0, 1)
+    def spread_normed(_, __):
+        for ky, kc in ((0, 1), (1, 0), (1, 1)):
+            copies.start(("n", ky, kc), normed_ref, normed_all.at[spot], ky=ky, kc=kc)
+
+    def cot_send(name, from_z, from_x, from_y, **partner):
+        held = cot_view(from_z, from_x, from_y)
+        source = held if from_z or from_x or from_y else cot_ref
+        copies.start(name, source, held, **partner)
+
+    def cot_z(kz, _):
+        cot_send(("cz", kz), 0, 0, 0, kz=kz)
+
+    def cot_relay(_, __):
+        copies.arrived(("cz", 2))
+        cot_send(("cz", 3), 2, 0, 0, kz=1)
+
+    def cot_x(kz, _):
+        if kz:
+            copies.arrived(("cz", kz))
+        cot_send(("cx", kz), kz, 0, 0, kx=1)
+        cot_send(("cs", kz, 0, 0), kz, 0, 0, kc=1)
+
+    def cot_y(kz, kx):
+        if kx:
+            copies.arrived(("cx", kz))
+        cot_send(("cy", kz, kx), kz, kx, 0, ky=1)
+        if kx:
+            cot_send(("cs", kz, 1, 0), kz, 1, 0, kc=1)
+
+    def cot_core(kz, kx):
+        copies.arrived(("cy", kz, kx))
+        cot_send(("cs", kz, kx, 1), kz, kx, 1, kc=1)
+
+    moves = {
+        SPREAD_Z: spread_z,
+        RELAY_Z: relay_z,
+        PASS_ON_X: pass_x,
+        SLICES: slices,
+        NORMED: spread_normed,
+        COT_Z: cot_z,
+        COT_RELAY: cot_relay,
+        COT_X: cot_x,
+        COT_Y: cot_y,
+        COT_CORE: cot_core,
+    }
+    for kind, a, b in OPENING_PLAN:
+        moves[kind](a, b)
     for keep in keeps:
         keep.wait()
     for name in copies.made:
-        if name[0] not in ("zi", "zo") :
-            copies.arrived(name)
+        copies.arrived(name)
     for name in copies.made:
         copies.sent(name)
 
 
-def opening(normed, att_in, att_out, shared_in, shared_out):
+def opening(normed, att_in, att_out, shared_in, shared_out, cotangent):
     rows, width = normed.shape
     parts, owner_width, heads_width = att_in.shape
     owners = lax.axis_size(EXPERT)
@@ -1424,13 +1700,14 @@
             jax.ShapeDtypeStruct((owners,) + att_out.shape, bf16),
             jax.ShapeDtypeStruct((2 * shared_part, width), bf16),
             jax.ShapeDtypeStruct((shared_part, width), bf16),
+            jax.ShapeDtypeStruct((rows * shards * owners, width), bf16),
         ),
-        in_specs=[anywhere] * 5,
-        out_specs=(anywhere,) * 5,
+        in_specs=[anywhere] * 6,
+        out_specs=(anywhere,) * 6,
         scratch_shapes=[
             pltpu.SemaphoreType.DMA((OPENING_COPIES,)),
             pltpu.SemaphoreType.DMA((OPENING_COPIES,)),
-            pltpu.SemaphoreType.DMA((5,)),
+            pltpu.SemaphoreType.DMA((6,)),
         ],
         compiler_params=pltpu.CompilerParams(
             collective_id=2, has_side_effects=True, vmem_limit_bytes=62 * 2**20
@@ -1439,7 +1716,7 @@
             flops=10**11, bytes_accessed=600 * 2**20, transcendentals=0
         ),
         name="opening",
-    )(normed, att_in, att_out, shared_in, shared_out)
+    )(normed, att_in, att_out, shared_in, shared_out, cotangent)
 
 
 def attention_forward(queries, keys_all, values, score_scale):
@@ -1485,7 +1762,6 @@
     expert_picks,
 ):
     bf16, f32 = jnp.bfloat16, jnp.float32
-    axes = (EXPERT, SHARD)
     local_rows, width = tokens.shape
     shards = lax.axis_size(SHARD)
     owners = lax.axis_size(EXPERT)
@@ -1513,15 +1789,14 @@
     small = small.reshape(small_rows, slice_rows)
     shared_blocks = shared_in.transpose(1, 2, 0).reshape(2, owners, shared_part, slice_rows)
     shared_blocks = shared_blocks.transpose(1, 0, 2, 3).reshape(owners, -1, slice_rows)
-    cot_all = lax.all_gather(cotangent, axes, axis=0, tiled=True)
-    normed_all, att_in, out_small, shared_win, shared_wout = opening(
+    normed_all, att_in, out_small, shared_win, shared_wout, cot_all = opening(
         first_low,
         attention_in.transpose(1, 0, 2),
         jnp.concatenate([attention_out, small], axis=0),
         shared_blocks,
         shared_out,
-    )
-    normed_all, att_in, cot_all = lax.optimization_barrier((normed_all, att_in, cot_all))
+        cotangent,
+    )
     att_out = out_small[:, : attention_out.shape[0]].transpose(1, 0, 2)
     att_out = att_out.reshape(attention_out.shape[0], width)
     small_all = out_small[:, attention_out.shape[0] :].reshape(owners, -1)
@@ -1542,27 +1817,14 @@
     attended, probs = attention_forward(queries, keys_all, values, score_scale)
     attended_low = attended.astype(bf16).reshape(seq_length, -1)
     attn_part = jnp.dot(attended_low, att_out, preferred_element_type=f32)
-    attn_local = lax.psum_scatter(
-        attn_part.astype(bf16), SHARD, scatter_dimension=0, tiled=True
-    ).astype(f32)
-    residual = inputs + attn_local
-    second_norm, second_factor = normalize(residual)
-    second_low = (second_norm * second_gain).astype(bf16)
-    logits = jnp.dot(second_low, router_full, preferred_element_type=f32)
-    route_probs = jax.nn.softmax(logits, axis=-1)
+    router_wide = jnp.concatenate([router_full.T, gate_full[None]], axis=0)
+    router_wide = jnp.pad(router_wide, ((0, EXTRA - experts - 1), (0, 0)))
     picked = jnp.sum(
         (
-            expert_picks[:, :, None] == jnp.arange(experts, dtype=jnp.int32)[None, None, :]
+            expert_picks[:, :, None] == jnp.arange(EXTRA, dtype=jnp.int32)[None, None, :]
         ).astype(f32),
         axis=1,
     )
-    shared_scale = jax.nn.sigmoid(jnp.dot(second_low, gate_full, preferred_element_type=f32))
-
-    weights_here = jnp.concatenate([picked * route_probs, shared_scale[:, None]], axis=1)
-    coarse = weights_here.astype(bf16)
-    fine = (weights_here - coarse.astype(f32)).astype(bf16)
-    filler = jnp.zeros((local_rows, EXTRA - 2 * (experts + 1)), bf16)
-    row_pack = jnp.concatenate([second_low, coarse, fine, filler], axis=1)
     units = owned * part + shared_part
     padded = -(-units // 128) * 128
     unit = jnp.arange(padded)
@@ -1572,8 +1834,17 @@
     spots = (kinds[None, :] == column[:, None]).astype(bf16)
     finer = jnp.where(unit < units, column + experts + 1, -1)
     select = (kinds[:, None] == column[None, :]) | (kinds[:, None] == finer[None, :])
-    output, back_local, rows_all, units_all = mixture(
-        row_pack,
+    (
+        output,
+        second_block,
+        residual_grad,
+        logit_grad,
+        second_gain_grad,
+        rows_all,
+        units_all,
+        residual_all,
+    ) = mixture(
+        attn_part.astype(bf16),
         cot_all,
         expert_in,
         shared_win,
@@ -1581,28 +1852,13 @@
         shared_wout,
         select.astype(bf16),
         spots,
-        residual,
+        tokens,
+        second_gain[None],
+        router_wide,
+        picked,
+        experts,
     )
     first_dims = (((0,), (0,)), ((), ()))
-    out_grad = cotangent.astype(f32)
-    pick_grads = back_local[:, width : width + experts] * picked
-    logit_grad = (
-        route_probs
-        * (pick_grads - jnp.sum(pick_grads * route_probs, axis=-1, keepdims=True))
-    ).astype(bf16)
-    gate_logit_grad = (
-        back_local[:, width + experts] * shared_scale * (1.0 - shared_scale)
-    ).astype(bf16)
-    local_back = lax.dot_general(
-        logit_grad, router_full, (((1,), (1,)), ((), ())), preferred_element_type=f32
-    )
-    local_back = local_back + gate_logit_grad.astype(f32)[:, None] * gate_full.astype(f32)[None]
-    second_grad = local_back + back_local[:, :width]
-    residual_back, second_gain_grad = norm_back(
-        second_grad, second_norm, second_factor, second_gain
-    )
-    residual_grad = out_grad + residual_back
-    residual_all = lax.all_gather(residual_grad.astype(bf16), SHARD, axis=0, tiled=True)
     att_out_grad = lax.dot_general(
         attended_low, residual_all, first_dims, preferred_element_type=f32
     )
@@ -1625,14 +1881,12 @@
     att_in_grad = jnp.einsum("sd,scf->cdf", normed_all, projected_grad, preferred_element_type=f32)
     att_bias_grad = jnp.sum(projected_grad.astype(f32), axis=0)
     first_part = jnp.einsum("scf,cdf->sd", projected_grad, att_in, preferred_element_type=f32)
-    first_grad = lax.psum_scatter(
-        first_part.astype(bf16), SHARD, scatter_dimension=0, tiled=True
-    ).astype(f32)
-    input_back, first_gain_grad = norm_back(first_grad, first_norm, first_factor, first_gain)
-    input_grad = residual_grad + input_back
-
-    vec_grads = jnp.concatenate([logit_grad, gate_logit_grad[:, None]], axis=1)
-    vec_grads = lax.dot_general(vec_grads, second_low, first_dims, preferred_element_type=f32)
+    vec_grads = lax.dot_general(
+        logit_grad[:, : experts + 1],
+        second_block[:, :width],
+        first_dims,
+        preferred_element_type=f32,
+    )
     bias_wide = jnp.zeros((3, shards, heads_here * head_dim), f32)
     bias_wide = lax.dynamic_update_slice_in_dim(
         bias_wide, att_bias_grad[:, None], lax.axis_index(SHARD), 1
@@ -1640,10 +1894,11 @@
     bias_rows = bias_wide.size // width
     first_bias = experts + 3
     small = jnp.concatenate(
-        [vec_grads, second_gain_grad[None], first_gain_grad[None], bias_wide.reshape(-1, width)]
+        [vec_grads, second_gain_grad, jnp.zeros((1, width), f32), bias_wide.reshape(-1, width)]
     )
     small = jnp.pad(small, ((0, -small.shape[0] % 8), (0, 0)))
     (
+        input_grad,
         att_in_local,
         att_out_local,
         summed,
@@ -1657,7 +1912,12 @@
         units_all,
         att_in_grad.astype(bf16),
         att_out_grad.astype(bf16),
+        first_part.astype(bf16),
         small,
+        tokens,
+        residual_grad,
+        first_gain[None],
+        experts + 2,
         owned,
         part,
         shared_part,

time: 936 us -> 731 us (0.78)
  waiting for transfers between devices: 90.7 us -> 0 us
  Pallas kernels: 701 us -> 627 us
  local copies, waits for them, and re-layouts: 38.5 us -> 25.1 us
  between operations: 14.9 us -> 1.54 us
  other arithmetic: 36 us -> 26 us
    pallas_call x1, Pallas kernels: 225 us -> 168 us  [opening(): pl.pallas_call(functools.partial(opening_kernel, (rows, owner_width, shar...]
    reduce_scatter x2 -> x0, waiting for transfers between devices: 47.2 us -> none  [the longest x1 28.6 us: local_gather(): lax.psum_scatter(attn_part.astype(bf16), SHARD, scatter_dimension=0, tile...]
    all_gather x2 -> x0, waiting for transfers between devices: 42.8 us -> none  [the longest x1 42.8 us: local_gather(): lax.all_gather(residual_grad.astype(bf16), SHARD, axis=0, tiled=True)]
    pallas_call x1, Pallas kernels: 181 us -> 163 us  [closing(): pl.pallas_call(functools.partial(closing_kernel, (width, owned, part, sha...]
  transfers between devices with their start and end apart: 4 -> 0, of which waited for: 3 -> 0; matrix products, arithmetic and copies ran while one was open for 3% -> 0% of each run, Pallas kernels for 24% -> 0%
where the time goes in v2:
time: 731 us; the launch traced here: 723 us
  Pallas kernels  627 us (86%)
  matrix products  44 us (6%)
  other arithmetic  26 us (4%)
  local copies, waits for them, and re-layouts  25.1 us (3%)
    pallas_call x1, Pallas kernels, mixture(): pl.pallas_call(functools.partial(mixture_kernel, (rows, seq, width, owned...  296 us
    pallas_call x1, Pallas kernels, opening(): pl.pallas_call(functools.partial(opening_kernel, (rows, owner_width, shar...  168 us
    pallas_call x1, Pallas kernels, closing(): pl.pallas_call(functools.partial(closing_kernel, (width, owned, part, sha...  163 us

profile of v2, /device:TPU:0, one launch (start us, length us, event | category | flops | bytes accessed | tf_op | source)
XLA Modules:
  0.0 723.5 jit_solution(6214864930958975399)
XLA Ops:
  0.7 3.8 copy.63
  4.5 1.2 copy.64
  5.9 1.0 fusion.13.normed_ref
  7.2 0.7 pad_maximum_fusion.1.att_out_ref
  8.0 167.9 %opening.1 = (bf16[512,2048]{1,0:T(8,128)(2,1)}, bf16[3,2048,512]{2,1,0:T(8,128)(2,1)}, bf16[8,544,256]{2,1,0:T(8,128)(2,1)}, bf16[352,2048]{1,0:T(8,128)(2,1)},...) custom-call(bf16[128,2048]{1,0:T(8,128)(2,1)} %fusion.13.normed_ref, bf16[3,256,512]{2,1,0:T(8,128)(2,1)} %bitcast.148, ...), custom_call_target="tpu_custom_call" | custom-call | flops 99999997952 | bytes 629145600 | tf_op jit(solution)/shard_map/opening/pallas_call | solution.py:1695
  175.9 0.9 slice_bitcast_fusion.3
  177.1 6.3 fusion.8
  183.9 0.5 fusion.37
  184.4 0.8 broadcast_multiply_fusion.2
  185.2 1.6 fusion.19
  186.8 0.8 iota_compare_fusion.1
  187.6 5.0 fusion.55
  192.5 3.6 convolution_convert_fusion.4
  196.3 2.6 copy.70
  198.9 4.3 convolution_convert_fusion.1.part_ref
  203.1 0.4 reshape.201
  203.8 0.8 fusion.25.router_ref
  204.6 0.8 fusion.29.select_ref
  205.4 0.9 fusion.30.place_ref
  206.2 0.8 convert_reduce_fusion.1.picked_ref
  207.0 296.2 %mixture.1 = (bf16[128,2048]{1,0:T(8,128)(2,1)}, bf16[128,2176]{1,0:T(8,128)(2,1)}, f32[128,2048]{1,0:T(8,128)}, bf16[128,128]{1,0:T(8,128)(2,1)}, f32[1,2048]{1...) custom-call(bf16[512,2048]{1,0:T(8,128)(2,1)} %convolution_convert_fusion.1.part_ref,, ...), custom_call_target="tpu_custom_call" | custom-call | flops 90194313216 | bytes 104857600 | tf_op jit(solution)/shard_map/mixture/pallas_call | solution.py:1031
  503.2 1.3 fusion.26
  504.5 3.7 convolution_convert_fusion.2
  508.2 2.0 multiply_reduce_fusion
  510.2 1.2 multiply_convert_fusion
  511.4 0.8 convolution_bitcast_fusion
  512.5 0.6 broadcast_multiply_fusion.1
  513.2 0.7 copy-done.10
  514.0 0.6 fusion.20
  514.6 0.8 convolution_convert_fusion.3
  516.0 0.7 pad.14.small_ref
  516.7 7.8 %bitcast_convert_fusion.first_ref = bf16[512,2048]{1,0:T(8,128)(2,1)} fusion(bf16[3,2048,512]{2,1,0:T(8,128)(2,1)} %get-tuple-element.36, bf16[512,1,512]{0,2,1:T(8,128)(2,1)S(1)} %bitcast.129, bf16[512,1,512]{0,2,1:T(8,128)(2,1)S(1)} %bitcast.123, bf16[512,1,512]{0,2,1:T(8,128)(2,1)S(1)} %bitcast.120), kind=kOutput, calls=%fused_computation.3 | convolution fusion | flops 3223846912 | bytes 9961472 | tf_op jit(solution)/shard_map/scf,cdf->sd/dot_general | solution.py:1883
  524.5 2.6 convolution_convert_fusion.att_out_ref
  527.1 5.4 convert_bitcast_fusion.1.att_in_ref
  532.5 162.7 %closing.1 = (f32[128,2048]{1,0:T(8,128)}, f32[3,256,512]{2,1,0:T(8,128)}, f32[512,256]{1,0:T(8,128)}, f32[24,2048]{1,0:T(8,128)}, bf16[1408,2048]{1,0:T(8,128)(...) custom-call(bf16[4096,2176]{1,0:T(8,128)(2,1)} %get-tuple-element.42.rows_ref, ...), custom_call_target="tpu_custom_call" | custom-call | flops 45097156608 | bytes 157286400 | tf_op jit(solution)/shard_map/closing/pallas_call | solution.py:1467
  695.2 8.8 %convert_bitcast_fusion = f32[2,2048,2,352]{1,3,2,0:T(8,128)} fusion(bf16[2,2,352,2048]{3,2,1,0:T(8,128)(2,1)} %bitcast.110), kind=kLoop, calls=%fused_computation.1 | loop fusion | flops 2883584 | bytes 17301504 | tf_op jit(solution)/shard_map/convert_element_type | solution.py:1926
  704.0 3.3 convert.33
  707.6 3.4 copy.80
  711.1 2.4 bitcast_convert_fusion.1
  713.5 1.0 slice.92
  714.6 0.6 constant_dynamic-slice_fusion
  715.2 1.3 dynamic-slice_bitcast_fusion
  716.5 1.5 fusion.54
  718.0 1.3 dynamic-slice.3
  719.3 0.8 copy.100
  720.1 1.0 copy.101
  721.1 1.1 copy.102
  722.2 0.8 copy.103
  (77 shorter events, 3.1 us)
Async XLA Ops:
  0.6 5.0 copy-start.4
  4.4 1.5 copy-start.14
  4.4 2.4 copy-start.15
  4.4 2.7 copy-start.17
  4.5 2.7 copy-start.19
  4.5 2.8 copy-start.13
  183.4 9.1 %copy-start = (f32[512,3,512]{0,2,1:T(8,128)}, f32[512,3,512]{0,2,1:T(8,128)S(1)}, u32[]{:S(2)}) copy-start(f32[512,3,512]{0,2,1:T(8,128)S(1)} %fusion.8) | copy-start | bytes 9437188
  192.5 3.6 copy-start.3
  196.3 2.6 copy-start.20
  203.1 3.1 copy-start.18
  504.5 3.7 copy-start.1
  510.2 1.2 copy-start.6
  511.4 1.0 copy-start.5
  513.0 1.0 copy-start.10
  514.6 1.3 copy-start.16
  516.7 7.8 %copy-start.21 = (bf16[512,2048]{1,0:T(8,128)(2,1)S(1)}, bf16[512,2048]{1,0:T(8,128)(2,1)}, u32[]{:S(2)}) copy-start(bf16[512,2048]{1,0:T(8,128)(2,1)} %get-tuple-element.44) | copy-start | bytes 6291460
  524.5 2.6 copy-start.22
  695.2 8.8 %copy-start.2 = (bf16[704,2048]{1,0:T(8,128)(2,1)S(1)}, bf16[704,2048]{1,0:T(8,128)(2,1)}, u32[]{:S(2)}) copy-start(bf16[704,2048]{1,0:T(8,128)(2,1)} %get-tuple-element.56) | copy-start | bytes 8650756
  704.0 3.3 copy-start.8
  711.0 8.3 %copy-start.11 = (bf16[128,2048]{1,0:T(8,128)(2,1)S(1)}, bf16[128,2048]{1,0:T(8,128)(2,1)}, u32[]{:S(2)}) copy-start(bf16[128,2048]{1,0:T(8,128)(2,1)} %get-tuple-element.131) | copy-start | bytes 1572868
  711.1 9.1 %copy-start.9 = (f32[128,2048]{1,0:T(8,128)S(1)}, f32[128,2048]{1,0:T(8,128)}, u32[]{:S(2)}) copy-start(f32[128,2048]{1,0:T(8,128)} %get-tuple-element.132) | copy-start | bytes 3145732
  713.5 7.6 %copy-start.7 = (f32[3,256,512]{2,1,0:T(8,128)S(1)}, f32[3,256,512]{2,1,0:T(8,128)}, u32[]{:S(2)}) copy-start(f32[3,256,512]{2,1,0:T(8,128)} %get-tuple-element.51) | copy-start | bytes 4718596
  720.1 2.1 copy-start.12

commit v3 on v2

--- a/solution.py
+++ b/solution.py
@@ -826,19 +826,28 @@
     copies.sent(("py", 0))
     own.start()
 
+    tile, wide = 256, 512
+
     def raise_tile(at, count):
         here, above = pl.ds(at, count), pl.ds(at + padded, count)
-        pair = jnp.concatenate([weight_in[here, :], weight_in[above, :]], axis=0)
-        raised = lax.dot_general(
-            rows_buf[:, pl.ds(0, width)], pair, NT_DIMS, preferred_element_type=f32
-        )
+        low_rows = rows_buf[:, pl.ds(0, width)]
+        if count == tile:
+            gate, up = (
+                lax.dot_general(
+                    low_rows, weight_in[at_rows, :], NT_DIMS, preferred_element_type=f32
+                )
+                for at_rows in (here, above)
+            )
+        else:
+            pair = jnp.concatenate([weight_in[here, :], weight_in[above, :]], axis=0)
+            raised = lax.dot_general(low_rows, pair, NT_DIMS, preferred_element_type=f32)
+            gate, up = raised[:, :count], raised[:, count:]
         back = lax.dot_general(
             cot_buf[...], weight_out[here, :], NT_DIMS, preferred_element_type=f32
         )
         scale = jnp.dot(
             rows_buf[:, pl.ds(width, EXTRA)], select_ref[:, here], preferred_element_type=f32
         )
-        gate, up = raised[:, :count], raised[:, count:]
         sigmoid_gate = jax.nn.sigmoid(gate)
         active = gate * sigmoid_gate
         hidden = active * up
@@ -848,11 +857,9 @@
         scaled = back * scale
         units_buf[:, pl.ds(at + 2 * padded, count)] = (hidden * scale).astype(bf16)
         units_buf[:, here] = (
-            scaled * up * sigmoid_gate * (1.0 + gate * (1.0 - sigmoid_gate))
+            scaled * up * (sigmoid_gate + active * (1.0 - sigmoid_gate))
         ).astype(bf16)
         units_buf[:, above] = (scaled * active).astype(bf16)
-
-    tile, wide = 256, 512
 
     tiles = padded // tile
     pieces = tiles + (1 if padded % tile else 0)

time: 731 us -> 731 us (level)
  no operation moved by 1% of the time
where the time goes in v3:
time: 731 us; the launch traced here: 723 us
  Pallas kernels  627 us (86%)
  matrix products  44 us (6%)
  other arithmetic  26 us (4%)
  local copies, waits for them, and re-layouts  25.1 us (3%)
    pallas_call x1, Pallas kernels, mixture(): pl.pallas_call(functools.partial(mixture_kernel, (rows, seq, width, owned...  296 us
    pallas_call x1, Pallas kernels, opening(): pl.pallas_call(functools.partial(opening_kernel, (rows, owner_width, shar...  168 us
    pallas_call x1, Pallas kernels, closing(): pl.pallas_call(functools.partial(closing_kernel, (width, owned, part, sha...  163 us

profile of v3, /device:TPU:0, one launch (start us, length us, event | category | flops | bytes accessed | tf_op | source)
XLA Modules:
  0.0 723.4 jit_solution(12085746499008866831)
XLA Ops:
  0.7 3.8 copy.63
  4.5 1.2 copy.64
  5.9 1.0 fusion.13.normed_ref
  7.2 0.7 pad_maximum_fusion.1.att_out_ref
  8.0 167.9 %opening.1 = (bf16[512,2048]{1,0:T(8,128)(2,1)}, bf16[3,2048,512]{2,1,0:T(8,128)(2,1)}, bf16[8,544,256]{2,1,0:T(8,128)(2,1)}, bf16[352,2048]{1,0:T(8,128)(2,1)},...) custom-call(bf16[128,2048]{1,0:T(8,128)(2,1)} %fusion.13.normed_ref, bf16[3,256,512]{2,1,0:T(8,128)(2,1)} %bitcast.148, ...), custom_call_target="tpu_custom_call" | custom-call | flops 99999997952 | bytes 629145600 | tf_op jit(solution)/shard_map/opening/pallas_call | solution.py:1702
  175.9 0.9 slice_bitcast_fusion.3
  177.1 6.3 fusion.8
  183.9 0.5 fusion.37
  184.4 0.8 broadcast_multiply_fusion.2
  185.2 1.6 fusion.19
  186.8 0.8 iota_compare_fusion.1
  187.6 5.0 fusion.55
  192.5 3.6 convolution_convert_fusion.4
  196.3 2.6 copy.70
  198.9 4.3 convolution_convert_fusion.1.part_ref
  203.1 0.4 reshape.201
  203.8 0.8 fusion.25.router_ref
  204.6 0.8 fusion.29.select_ref
  205.4 0.9 fusion.30.place_ref
  206.2 0.8 convert_reduce_fusion.1.picked_ref
  207.0 296.2 %mixture.1 = (bf16[128,2048]{1,0:T(8,128)(2,1)}, bf16[128,2176]{1,0:T(8,128)(2,1)}, f32[128,2048]{1,0:T(8,128)}, bf16[128,128]{1,0:T(8,128)(2,1)}, f32[1,2048]{1...) custom-call(bf16[512,2048]{1,0:T(8,128)(2,1)} %convolution_convert_fusion.1.part_ref,, ...), custom_call_target="tpu_custom_call" | custom-call | flops 90194313216 | bytes 104857600 | tf_op jit(solution)/shard_map/mixture/pallas_call | solution.py:1038
  503.2 1.3 fusion.26
  504.4 3.7 convolution_convert_fusion.2
  508.1 2.0 multiply_reduce_fusion
  510.2 1.2 multiply_convert_fusion
  511.4 0.8 convolution_bitcast_fusion
  512.4 0.6 broadcast_multiply_fusion.1
  513.2 0.7 copy-done.10
  513.9 0.6 fusion.20
  514.5 0.8 convolution_convert_fusion.3
  516.0 0.7 pad.14.small_ref
  516.7 7.8 %bitcast_convert_fusion.first_ref = bf16[512,2048]{1,0:T(8,128)(2,1)} fusion(bf16[3,2048,512]{2,1,0:T(8,128)(2,1)} %get-tuple-element.36, bf16[512,1,512]{0,2,1:T(8,128)(2,1)S(1)} %bitcast.129, bf16[512,1,512]{0,2,1:T(8,128)(2,1)S(1)} %bitcast.123, bf16[512,1,512]{0,2,1:T(8,128)(2,1)S(1)} %bitcast.120), kind=kOutput, calls=%fused_computation.3 | convolution fusion | flops 3223846912 | bytes 9961472 | tf_op jit(solution)/shard_map/scf,cdf->sd/dot_general | solution.py:1890
  524.4 2.6 convolution_convert_fusion.att_out_ref
  527.0 5.4 convert_bitcast_fusion.1.att_in_ref
  532.4 162.7 %closing.1 = (f32[128,2048]{1,0:T(8,128)}, f32[3,256,512]{2,1,0:T(8,128)}, f32[512,256]{1,0:T(8,128)}, f32[24,2048]{1,0:T(8,128)}, bf16[1408,2048]{1,0:T(8,128)(...) custom-call(bf16[4096,2176]{1,0:T(8,128)(2,1)} %get-tuple-element.42.rows_ref, ...), custom_call_target="tpu_custom_call" | custom-call | flops 45097156608 | bytes 157286400 | tf_op jit(solution)/shard_map/closing/pallas_call | solution.py:1474
  695.1 8.8 %convert_bitcast_fusion = f32[2,2048,2,352]{1,3,2,0:T(8,128)} fusion(bf16[2,2,352,2048]{3,2,1,0:T(8,128)(2,1)} %bitcast.110), kind=kLoop, calls=%fused_computation.1 | loop fusion | flops 2883584 | bytes 17301504 | tf_op jit(solution)/shard_map/convert_element_type | solution.py:1933
  704.0 3.3 convert.33
  707.6 3.4 copy.80
  711.0 2.4 bitcast_convert_fusion.1
  713.4 1.0 slice.92
  714.5 0.6 constant_dynamic-slice_fusion
  715.1 1.3 dynamic-slice_bitcast_fusion
  716.5 1.5 fusion.54
  718.0 1.3 dynamic-slice.3
  719.3 0.8 copy.100
  720.1 1.0 copy.101
  721.0 1.1 copy.102
  722.2 0.8 copy.103
  (77 shorter events, 3.1 us)
Async XLA Ops:
  0.6 5.0 copy-start.4
  4.4 1.5 copy-start.14
  4.4 2.4 copy-start.15
  4.4 2.7 copy-start.17
  4.5 2.7 copy-start.19
  4.5 2.8 copy-start.13
  183.4 9.1 %copy-start = (f32[512,3,512]{0,2,1:T(8,128)}, f32[512,3,512]{0,2,1:T(8,128)S(1)}, u32[]{:S(2)}) copy-start(f32[512,3,512]{0,2,1:T(8,128)S(1)} %fusion.8) | copy-start | bytes 9437188
  192.5 3.6 copy-start.3
  196.3 2.6 copy-start.20
  203.1 3.1 copy-start.18
  504.4 3.7 copy-start.1
  510.1 1.2 copy-start.6
  511.4 1.0 copy-start.5
  513.0 1.0 copy-start.10
  514.5 1.3 copy-start.16
  516.6 7.8 %copy-start.21 = (bf16[512,2048]{1,0:T(8,128)(2,1)S(1)}, bf16[512,2048]{1,0:T(8,128)(2,1)}, u32[]{:S(2)}) copy-start(bf16[512,2048]{1,0:T(8,128)(2,1)} %get-tuple-element.44) | copy-start | bytes 6291460
  524.4 2.6 copy-start.22
  695.1 8.8 %copy-start.2 = (bf16[704,2048]{1,0:T(8,128)(2,1)S(1)}, bf16[704,2048]{1,0:T(8,128)(2,1)}, u32[]{:S(2)}) copy-start(bf16[704,2048]{1,0:T(8,128)(2,1)} %get-tuple-element.56) | copy-start | bytes 8650756
  704.0 3.3 copy-start.8
  711.0 8.3 %copy-start.11 = (bf16[128,2048]{1,0:T(8,128)(2,1)S(1)}, bf16[128,2048]{1,0:T(8,128)(2,1)}, u32[]{:S(2)}) copy-start(bf16[128,2048]{1,0:T(8,128)(2,1)} %get-tuple-element.131) | copy-start | bytes 1572868
  711.0 9.1 %copy-start.9 = (f32[128,2048]{1,0:T(8,128)S(1)}, f32[128,2048]{1,0:T(8,128)}, u32[]{:S(2)}) copy-start(f32[128,2048]{1,0:T(8,128)} %get-tuple-element.132) | copy-start | bytes 3145732
  713.4 7.6 %copy-start.7 = (f32[3,256,512]{2,1,0:T(8,128)S(1)}, f32[3,256,512]{2,1,0:T(8,128)}, u32[]{:S(2)}) copy-start(f32[3,256,512]{2,1,0:T(8,128)} %get-tuple-element.51) | copy-start | bytes 4718596
  720.1 2.1 copy-start.12
